TPU v7x, 32 devices: a whole 2x2x4 slice. The times are simulated.
32 devices in a mesh: group: 2 (over y), dp: 8 (over z, x), tensor: 2 (over core).
Axes of the slice: x: 2, y: 2, z: 4, core: 2. Of those that a mesh axis runs over, the one named last changes fastest.
Arguments:
- queries: bfloat16 [64, 32, 4096], P(('group', 'dp'), None, 'tensor'), parts along dimension 0, may hold values from -17 to 17
- response_cache: bfloat16 [64, 32, 2, 512], P(('group', 'dp'), None, None, 'tensor'), parts along dimension 0, may hold values from -6 to 6
- prefix_cache: bfloat16 [16, 224, 2, 512], P(('group', 'dp'), None, None, 'tensor'), parts along dimension 0, may hold values from -8 to 8
- upstream: bfloat16 [64, 32, 4096], P(('group', 'dp'), None, 'tensor'), parts along dimension 0, may hold values from -6 to 6
- reward_probe: float32 [4096], P('tensor'), may hold values from -1.5 to 1.5
- slot_offsets: int32 [16, 4], P(('group', 'dp')), parts along dimension 0, may hold values from -2 to 2, as said below
- partner: int32 [64], P('group'), parts along dimension 0, may hold values from 0 to 31, as said below
- labels: int32 [64], P('group'), parts along dimension 0, may hold values from 0 to 2
Outputs:
- rewards: float32 [64], P(('group', 'dp')), parts along dimension 0
- pair_loss: float32 [2], P('group'), parts along dimension 0
- grad_queries: bfloat16 [64, 32, 4096], P(('group', 'dp'), None, 'tensor'), parts along dimension 0
- grad_response: bfloat16 [64, 32, 2, 512], P(('group', 'dp'), None, None, 'tensor'), parts along dimension 0
- grad_prefix: bfloat16 [16, 224, 2, 512], P(('group', 'dp'), None, None, 'tensor'), parts along dimension 0
There are 2 independent parts, one for each index of `group`. A program takes and returns all parts, laid end to end along the dimension named above; an argument that names none is the same for every part. Nothing has to cross between parts.
Inputs may be any that keep to these rules, and one draw needn't show every extreme that they name: `slot_offsets`: slots 0 and 1 of every device have offset 0. partner[i] differs from i and has the same prompt; the responses of one prompt name each other once around a cycle.
All inputs are finite; a program needn't handle non-finite values.
Results may differ from a plain program's by a relative error of at most 0.011.
Values may be sent and summed in bfloat16 or wider, within the bound.
A program may use at most 64 MiB of HBM per device.

v0:
```python
import math

import jax
import jax.numpy as jnp
from jax import lax
from jax.sharding import PartitionSpec as P

HD = 128
SPAN = 2


def passed_along(block, axis, distance):
    devices = range(lax.axis_size(axis))
    route = [((i - distance) % len(devices), i) for i in devices]
    return lax.ppermute(block, axis, route)


def neighbour(block_data, shift_by):
    return passed_along(block_data, "dp", shift_by)


def send_home(block_data, shift_by):
    return passed_along(block_data, "dp", shift_by)


def davidson(reward_all, partner, labels):
    second = reward_all[partner]
    middle = 0.5 * (reward_all + second)
    exp_first = jnp.exp(reward_all)
    exp_second = jnp.exp(second)
    exp_middle = jnp.exp(middle)
    totals = exp_first + exp_second + exp_middle
    chosen = jnp.where(labels == 0, reward_all, jnp.where(labels == 1, second, middle))
    loss_value = jnp.mean(jnp.log(totals) - chosen).reshape(1)
    tie_share = 0.5 * exp_middle / totals
    half_tie = jnp.where(labels == 2, 0.5, 0.0)
    grad_first = exp_first / totals + tie_share - jnp.where(labels == 0, 1.0, 0.0) - half_tie
    grad_second = exp_second / totals + tie_share - jnp.where(labels == 1, 1.0, 0.0) - half_tie
    indices = jnp.arange(reward_all.shape[0], dtype=jnp.int32)
    reward_grad = (
        jnp.zeros_like(reward_all).at[indices].add(grad_first).at[partner].add(grad_second)
    )
    return (loss_value, reward_grad)


def per_device(
    queries, response_cache, prefix_cache, upstream, reward_probe, slot_offsets, partner, labels
):
    slot_count, row_count, query_width = queries.shape
    kv_width = response_cache.shape[3]
    kv_heads = kv_width // HD
    group_size = query_width // HD // kv_heads
    prefix_len = prefix_cache.shape[1]
    pieces = []
    for reach_by in range(-SPAN, SPAN + 1):
        pieces.append(prefix_cache if reach_by == 0 else neighbour(prefix_cache, -reach_by))
    nearby = jnp.concatenate(pieces, axis=0)
    slot_index = slot_offsets[0] + SPAN
    chosen_prefix = nearby[slot_index]
    key_rows = jnp.concatenate([chosen_prefix, response_cache], axis=1)
    total_keys = key_rows.shape[1]
    key_part = key_rows[:, :, 0].reshape(slot_count, total_keys, kv_heads, HD)
    value_part = key_rows[:, :, 1].reshape(slot_count, total_keys, kv_heads, HD)
    query_part = queries.reshape(slot_count, row_count, kv_heads, group_size, HD)
    score_scale = 1.0 / math.sqrt(HD)
    scores = (
        jnp.einsum("rtkgd,rnkd->rkgtn", query_part, key_part, preferred_element_type=jnp.float32)
        * score_scale
    )
    row_ids = lax.broadcasted_iota(jnp.int32, (row_count, total_keys), 0)
    col_ids = lax.broadcasted_iota(jnp.int32, (row_count, total_keys), 1)
    visible = (col_ids < prefix_len) | (col_ids - prefix_len <= row_ids)
    scores = jnp.where(visible, scores, -1e30)
    row_top = jnp.max(scores, axis=-1, keepdims=True)
    exp_scores = jnp.exp(scores - row_top)
    weights = exp_scores / jnp.sum(exp_scores, axis=-1, keepdims=True)
    weights_low = weights.astype(jnp.bfloat16)
    attended = jnp.einsum(
        "rkgtn,rnkd->rtkgd", weights_low, value_part, preferred_element_type=jnp.float32
    )
    partial_reward = jnp.sum(
        attended.reshape(slot_count, row_count, query_width)[:, -1] * reward_probe, axis=-1
    )
    own_rewards = lax.psum(partial_reward, "tensor")
    reward_table = lax.all_gather(own_rewards, "dp", axis=0, tiled=True)
    loss_value, reward_grad = davidson(reward_table, partner, labels)
    own_grad = lax.dynamic_slice_in_dim(reward_grad, lax.axis_index("dp") * slot_count, slot_count)
    d_attended = (
        upstream.astype(jnp.float32)
        .at[:, -1]
        .add(own_grad[:, None] * reward_probe)
        .astype(jnp.bfloat16)
    )
    d_part = d_attended.reshape(slot_count, row_count, kv_heads, group_size, HD)
    d_weights = jnp.einsum(
        "rtkgd,rnkd->rkgtn", d_part, value_part, preferred_element_type=jnp.float32
    )
    row_delta = jnp.transpose(
        jnp.sum(d_part.astype(jnp.float32) * attended, axis=-1), (0, 2, 3, 1)
    )[..., None]
    d_scores = (weights * (d_weights - row_delta) * score_scale).astype(jnp.bfloat16)
    d_query = jnp.einsum(
        "rkgtn,rnkd->rtkgd", d_scores, key_part, preferred_element_type=jnp.float32
    )
    grad_queries = d_query.reshape(slot_count, row_count, query_width).astype(jnp.bfloat16)
    d_key = jnp.einsum(
        "rkgtn,rtkgd->rnkd", d_scores, query_part, preferred_element_type=jnp.float32
    )
    d_value = jnp.einsum(
        "rkgtn,rtkgd->rnkd", weights_low, d_part, preferred_element_type=jnp.float32
    )
    d_rows = jnp.stack(
        [
            d_key.reshape(slot_count, total_keys, kv_width),
            d_value.reshape(slot_count, total_keys, kv_width),
        ],
        axis=2,
    )
    grad_response = d_rows[:, prefix_len:].astype(jnp.bfloat16)
    reach_count = 2 * SPAN + 1
    selector = (slot_index[:, None] == jnp.arange(reach_count, dtype=jnp.int32)[None, :]).astype(
        jnp.float32
    )
    by_reach = jnp.einsum(
        "rm,rlck->mlck", selector, d_rows[:, :prefix_len], precision=lax.Precision.HIGHEST
    ).astype(jnp.bfloat16)
    prefix_total = by_reach[SPAN].astype(jnp.float32)
    for reach_by in range(-SPAN, SPAN + 1):
        if reach_by != 0:
            arrived = send_home(by_reach[reach_by + SPAN][None], reach_by)
            prefix_total = prefix_total + arrived[0].astype(jnp.float32)
    grad_prefix = prefix_total[None].astype(jnp.bfloat16)
    return (own_rewards, loss_value, grad_queries, grad_response, grad_prefix)


def solution(mesh):
    in_specs = (
        P(("group", "dp"), None, "tensor"),
        P(("group", "dp"), None, None, "tensor"),
        P(("group", "dp"), None, None, "tensor"),
        P(("group", "dp"), None, "tensor"),
        P("tensor"),
        P(("group", "dp"), None),
        P("group"),
        P("group"),
    )
    out_specs = (
        P(("group", "dp")),
        P("group"),
        P(("group", "dp"), None, "tensor"),
        P(("group", "dp"), None, None, "tensor"),
        P(("group", "dp"), None, None, "tensor"),
    )
    return jax.shard_map(
        per_device, mesh=mesh, in_specs=in_specs, out_specs=out_specs, check_vma=False
    )
```

profile of v0, /device:TPU:0, one launch (start us, length us, event | category | flops | bytes accessed | tf_op | source)
XLA Modules:
  0.0 109.7 jit_solution(9196357513931993248)
XLA Ops:
  0.7 1.0 copy.35
  1.7 3.1 %collective-permute-start = (bf16[1,224,2,256]{3,1,2,0:T(8,128)(2,1)S(1)}, bf16[1,224,2,256]{3,1,2,0:T(8,128)(2,1)}, u32[]{:S(2)}, u32[]{:S(2)}) collective-permute-start(bf16[1,224,2,256]{3,1,2,0:T(8,128)(2,1)S(1)} %copy.35), channel_id=1, source_target_pairs={{12,0},{14,2},{0,4},{2,6},{4,8},{6,10},{8,12},{10,14},{13,1},{15,3... | collective-permute-start | bytes 688136 | tf_op jit(solution)/shard_map/ppermute | solution.py:15
  4.8 1.5 %collective-permute-start.1 = (bf16[1,224,2,256]{3,1,2,0:T(8,128)(2,1)S(1)}, bf16[1,224,2,256]{3,1,2,0:T(8,128)(2,1)S(1)}, u32[]{:S(2)}, u32[]{:S(2)}) collective-permute-start(bf16[1,224,2,256]{3,1,2,0:T(8,128)(2,1)S(1)} %copy.35), channel_id=1, source_target_pairs={{14,0},{0,2},{2,4},{4,6},{6,8},{8,10},{10,12},{12,14},{15,1},{1,3}... | collective-permute-start | bytes 688136 | tf_op jit(solution)/shard_map/ppermute | solution.py:15
  6.3 3.2 %collective-permute-start.2 = (bf16[1,224,2,256]{3,1,2,0:T(8,128)(2,1)S(1)}, bf16[1,224,2,256]{3,1,2,0:T(8,128)(2,1)S(1)}, u32[]{:S(2)}, u32[]{:S(2)}) collective-permute-start(bf16[1,224,2,256]{3,1,2,0:T(8,128)(2,1)S(1)} %copy.35), channel_id=1, source_target_pairs={{2,0},{4,2},{6,4},{8,6},{10,8},{12,10},{14,12},{0,14},{3,1},{5,3},... | collective-permute-start | bytes 688136 | tf_op jit(solution)/shard_map/ppermute | solution.py:15
  11.8 1.1 %copy.75 = bf16[16,8,16,128]{3,2,1,0:T(8,128)(2,1)S(1)} copy(bf16[16,8,16,128]{3,1,2,0:T(8,128)(2,1)} %bitcast.94) | data formatting | bytes 1048576
  14.4 1.6 %constant_dynamic-update-slice_fusion.4 = bf16[5,224,2,256]{3,1,2,0:T(8,128)(2,1)} fusion(bf16[1,224,2,256]{3,1,2,0:T(8,128)(2,1)} %collective-permute-done), kind=kLoop, calls=%fused_computation.52 | loop fusion | bytes 458752
  16.0 3.4 %collective-permute-done.1 = bf16[1,224,2,256]{3,1,2,0:T(8,128)(2,1)S(1)} collective-permute-done((bf16[1,224,2,256]{3,1,2,0:T(8,128)(2,1)S(1)}, bf16[1,224,2,256]{3,1,2,0:T(8,128)(2,1)S(1)}, u32[]{:S(2)}, u32[]{:S(2)}) %collective-permute-start.1) | collective-permute-done | bytes 229408 | tf_op jit(solution)/shard_map/ppermute | solution.py:15
  22.9 1.9 %gather_fusion = bf16[4,224,2,256]{3,1,2,0:T(8,128)(2,1)S(1)} fusion(bf16[5,224,2,256]{3,1,2,0:T(8,128)(2,1)} %constant_dynamic-update-slice_fusion, s32[1024]{0:T(1024)S(1)} %pad_clamp_fusion.1), kind=kCustom, calls=%fused_computation | custom fusion | bytes 1835024 | tf_op jit(solution)/shard_map/gather | solution.py:59
  25.0 1.0 copy.41
  26.2 2.1 %fusion.52 = (f32[4,2,8,32]{3,2,1,0:T(8,128)S(1)}, f32[4,2,8,32,256]{4,3,2,1,0:T(8,128)}) fusion(pred[32,256]{1,0:T(8,128)(4,1)S(1)} %fusion.31, bf16[4,256,2,128,1]{1,3,4,2,0:T(8,128)(2,1)S(1)} %bitcast.92, bf16[4,32,2,8,128]{4,3,2,1,0:T(8,128)(2,1)S(1)} %bitcast.87), kind=kOutput, calls=%fused_computation.87 | convolution fusion | flops 136315136 | bytes 3162112 | tf_op jit(solution)/shard_map/sub | solution.py:75
  28.3 2.0 %fusion.14 = bf16[4,2,8,32,256]{4,3,2,1,0:T(8,128)(2,1)S(1)} fusion(f32[4,2,8,32,256]{4,3,2,1,0:T(8,128)} %get-tuple-element.43, f32[4,2,8,32]{3,2,1,0:T(8,128)S(1)} %get-tuple-element.42), kind=kLoop, calls=%fused_computation.28 | loop fusion | flops 1048576 | bytes 3153920 | tf_op jit(solution)/shard_map/convert_element_type | solution.py:77
  30.8 1.6 %copy.46 = f32[4,32,2,8,128]{4,3,2,1,0:T(8,128)} copy(f32[4,32,2,8,128]{4,1,3,2,0:T(8,128)S(1)} %convolution_bitcast_fusion) | data formatting | bytes 2097152 | tf_op jit(solution)/shard_map/rkgtn,rnkd->rtkgd/transpose | solution.py:78
  32.4 2.4 %reshape.121 = f32[4,32,2048]{2,1,0:T(8,128)} reshape(f32[4,32,2,8,128]{4,3,2,1,0:T(8,128)} %copy.46) | data formatting | bytes 2097152 | tf_op jit(solution)/shard_map/reshape | solution.py:82
  34.8 1.0 slice.70
  35.9 2.5 %psum.7 = f32[4]{0:T(128)S(1)} all-reduce(f32[4]{0:T(128)S(1)} %fusion.30), channel_id=1, replica_groups=mesh['group'=2,'dp'=8,'tensor'=2] {'tensor'}, use_global_device_ids=true, to_apply=%region_3.4 | all-reduce | flops 4 | bytes 32 | tf_op jit(solution)/shard_map/psum | solution.py:84
  38.6 19.7 %all-reduce = f32[32]{0:T(128)S(1)} all-reduce(f32[32]{0:T(128)S(1)} %dynamic-update-slice.3), channel_id=1, replica_groups=mesh['group'=2,'dp'=8,'tensor'=2] {'dp'}, use_global_device_ids=true, to_apply=%add | all-reduce | flops 32 | bytes 256
  60.4 0.8 scatter_fusion
  62.3 0.8 fusion.9
  63.6 0.8 fusion.3
  64.8 2.4 %fusion.17 = f32[4,2,256,128,1]{2,3,4,1,0:T(8,128)} fusion(bf16[4,2,8,32,256]{4,3,2,1,0:T(8,128)(2,1)S(1)} %fusion.3, bf16[4,32,2,8,128]{4,3,2,1,0:T(8,128)(2,1)} %bitcast.88), kind=kOutput, calls=%fused_computation.31 | convolution fusion | flops 134217728 | bytes 2621440 | tf_op jit(solution)/shard_map/rkgtn,rtkgd->rnkd/dot_general | solution.py:106
  67.3 1.6 %copy.55 = f32[4,256,1,256]{3,0,2,1:T(4,128)S(1)} copy(f32[4,256,1,256]{1,3,0,2:T(8,128)} %bitcast.86) | data formatting | bytes 2097152 | tf_op jit(solution)/shard_map/stack;reshape | solution.py:112
  68.9 2.5 %fusion.7 = bf16[5,224,2,256]{3,0,2,1:T(8,128)(2,1)S(1)} fusion(f32[4,256,1,256]{3,0,2,1:T(4,128)S(1)} %copy.56, f32[4,256,1,256]{3,0,2,1:T(4,128)S(1)} %copy.55, s32[4]{0:T(128)S(1)} %add_bitcast_fusion), kind=kOutput, calls=%fused_computation.17 | convolution fusion | flops 28557332 | bytes 3244048 | tf_op jit(solution)/shard_map/rm,rlck->mlck/dot_general | solution.py:124
  71.5 2.5 %fusion.50 = (bf16[1,224,2,256]{3,0,2,1:T(2,128)(2,1)}, bf16[1,224,2,256]{3,0,2,1:T(2,128)(2,1)}, bf16[1,224,2,256]{3,0,2,1:T(2,128)(2,1)}, bf16[1,224,2,256]{3,0,2,1:T(2,128)(2,1)}) fusion(bf16[5,224,2,256]{3,0,2,1:T(8,128)(2,1)S(1)} %fusion.7), kind=kLoop, calls=%fused_computation.85 | loop fusion | bytes 1835008 | tf_op jit(solution)/shard_map/slice | solution.py:130
  74.0 1.8 %collective-permute-start.6 = (bf16[1,224,2,256]{3,0,2,1:T(2,128)(2,1)}, bf16[1,224,2,256]{3,0,2,1:T(2,128)(2,1)}, u32[]{:S(2)}, u32[]{:S(2)}) collective-permute-start(bf16[1,224,2,256]{3,0,2,1:T(2,128)(2,1)} %get-tuple-element.36), channel_id=1, source_target_pairs={{14,0},{0,2},{2,4},{4,6},{6,8},{8,10},{10,12},{12,14},{15,1},{1,3}... | collective-permute-start | bytes 688136 | tf_op jit(solution)/shard_map/ppermute | solution.py:15
  75.8 3.3 %collective-permute-start.5 = (bf16[1,224,2,256]{3,0,2,1:T(2,128)(2,1)}, bf16[1,224,2,256]{3,0,2,1:T(2,128)(2,1)}, u32[]{:S(2)}, u32[]{:S(2)}) collective-permute-start(bf16[1,224,2,256]{3,0,2,1:T(2,128)(2,1)} %get-tuple-element.37), channel_id=1, source_target_pairs={{2,0},{4,2},{6,4},{8,6},{10,8},{12,10},{14,12},{0,14},{3,1},{5,3},... | collective-permute-start | bytes 688136 | tf_op jit(solution)/shard_map/ppermute | solution.py:15
  79.1 1.7 %collective-permute-start.4 = (bf16[1,224,2,256]{3,0,2,1:T(2,128)(2,1)}, bf16[1,224,2,256]{3,0,2,1:T(2,128)(2,1)}, u32[]{:S(2)}, u32[]{:S(2)}) collective-permute-start(bf16[1,224,2,256]{3,0,2,1:T(2,128)(2,1)} %get-tuple-element.34), channel_id=1, source_target_pairs={{4,0},{6,2},{8,4},{10,6},{12,8},{14,10},{0,12},{2,14},{5,1},{7,3},... | collective-permute-start | bytes 688136 | tf_op jit(solution)/shard_map/ppermute | solution.py:15
  81.4 1.0 convert_element_type.61
  83.9 5.7 %collective-permute-done.7 = bf16[1,224,2,256]{3,0,2,1:T(2,128)(2,1)} collective-permute-done((bf16[1,224,2,256]{3,0,2,1:T(2,128)(2,1)}, bf16[1,224,2,256]{3,0,2,1:T(2,128)(2,1)}, u32[]{:S(2)}, u32[]{:S(2)}) %collective-permute-start.7) | collective-permute-done | bytes 229408 | tf_op jit(solution)/shard_map/ppermute | solution.py:15
  89.6 11.1 %collective-permute-done.6 = bf16[1,224,2,256]{3,0,2,1:T(2,128)(2,1)} collective-permute-done((bf16[1,224,2,256]{3,0,2,1:T(2,128)(2,1)}, bf16[1,224,2,256]{3,0,2,1:T(2,128)(2,1)}, u32[]{:S(2)}, u32[]{:S(2)}) %collective-permute-start.6) | collective-permute-done | bytes 229408 | tf_op jit(solution)/shard_map/ppermute | solution.py:15
  100.7 3.5 %collective-permute-done.4 = bf16[1,224,2,256]{3,0,2,1:T(2,128)(2,1)} collective-permute-done((bf16[1,224,2,256]{3,0,2,1:T(2,128)(2,1)}, bf16[1,224,2,256]{3,0,2,1:T(2,128)(2,1)}, u32[]{:S(2)}, u32[]{:S(2)}) %collective-permute-start.4) | collective-permute-done | bytes 229408 | tf_op jit(solution)/shard_map/ppermute | solution.py:15
  104.1 3.5 %add_convert_fusion = bf16[1,224,2,256]{3,0,2,1:T(2,128)(2,1)S(1)} fusion(bf16[1,224,2,256]{3,0,2,1:T(2,128)(2,1)} %collective-permute-done.7, bf16[1,224,2,256]{3,0,2,1:T(2,128)(2,1)} %collective-permute-done.6, bf16[1,224,2,256]{3,0,2,1:T(2,128)(2,1)} %collective-permute-done.5, bf16[1,224,2,256]{3,0,2,1:T(2,128)(2,1)} %collective-permute-done.4, ...), kind=kLoop, calls=%fused_computation.39 | loop fusion | flops 1146880 | bytes 1376256 | tf_op jit(solution)/shard_map/convert_element_type | solution.py:132
  107.7 0.9 copy.58
  (72 shorter events, 13.4 us)
Async XLA Ops:
  0.6 12.4 %copy-start.13 = (u32[32]{0:T(128)S(1)}, u32[32]{0:T(128)}, u32[]{:S(2)}) copy-start(u32[32]{0:T(128)} %constant.80) | copy-start | bytes 388
  0.6 12.3 %copy-start.8 = (bf16[4,32,2048]{2,1,0:T(8,128)(2,1)S(1)}, bf16[4,32,2048]{2,1,0:T(8,128)(2,1)}, u32[]{:S(2)}) copy-start(bf16[4,32,2048]{2,1,0:T(8,128)(2,1)} %param.13) | copy-start | bytes 1572868
  1.7 18.4 %copy-start.7 = (bf16[1,224,2,256]{3,2,1,0:T(2,128)(2,1)S(1)}, bf16[1,224,2,256]{3,2,1,0:T(2,128)(2,1)}, u32[]{:S(2)}) copy-start(bf16[1,224,2,256]{3,2,1,0:T(2,128)(2,1)} %param.12) | copy-start | bytes 688132
  1.7 12.7 %collective-permute-start = (bf16[1,224,2,256]{3,1,2,0:T(8,128)(2,1)S(1)}, bf16[1,224,2,256]{3,1,2,0:T(8,128)(2,1)}, u32[]{:S(2)}, u32[]{:S(2)}) collective-permute-start(bf16[1,224,2,256]{3,1,2,0:T(8,128)(2,1)S(1)} %copy.35), channel_id=1, source_target_pairs={{12,0},{14,2},{0,4},{2,6},{4,8},{6,10},{8,12},{10,14},{13,1},{15,3... | collective-permute-start | bytes 688136 | tf_op jit(solution)/shard_map/ppermute | solution.py:15
  4.8 14.6 %collective-permute-start.1 = (bf16[1,224,2,256]{3,1,2,0:T(8,128)(2,1)S(1)}, bf16[1,224,2,256]{3,1,2,0:T(8,128)(2,1)S(1)}, u32[]{:S(2)}, u32[]{:S(2)}) collective-permute-start(bf16[1,224,2,256]{3,1,2,0:T(8,128)(2,1)S(1)} %copy.35), channel_id=1, source_target_pairs={{14,0},{0,2},{2,4},{4,6},{6,8},{8,10},{10,12},{12,14},{15,1},{1,3}... | collective-permute-start | bytes 688136 | tf_op jit(solution)/shard_map/ppermute | solution.py:15
  6.3 14.5 %collective-permute-start.2 = (bf16[1,224,2,256]{3,1,2,0:T(8,128)(2,1)S(1)}, bf16[1,224,2,256]{3,1,2,0:T(8,128)(2,1)S(1)}, u32[]{:S(2)}, u32[]{:S(2)}) collective-permute-start(bf16[1,224,2,256]{3,1,2,0:T(8,128)(2,1)S(1)} %copy.35), channel_id=1, source_target_pairs={{2,0},{4,2},{6,4},{8,6},{10,8},{12,10},{14,12},{0,14},{3,1},{5,3},... | collective-permute-start | bytes 688136 | tf_op jit(solution)/shard_map/ppermute | solution.py:15
  9.5 12.7 %collective-permute-start.3 = (bf16[1,224,2,256]{3,1,2,0:T(8,128)(2,1)S(1)}, bf16[1,224,2,256]{3,1,2,0:T(8,128)(2,1)S(1)}, u32[]{:S(2)}, u32[]{:S(2)}) collective-permute-start(bf16[1,224,2,256]{3,1,2,0:T(8,128)(2,1)S(1)} %copy.35), channel_id=1, source_target_pairs={{4,0},{6,2},{8,4},{10,6},{12,8},{14,10},{0,12},{2,14},{5,1},{7,3},... | collective-permute-start | bytes 688136 | tf_op jit(solution)/shard_map/ppermute | solution.py:15
  12.9 13.3 %copy-start.1 = (bf16[16,8,16,128]{3,2,1,0:T(8,128)(2,1)}, bf16[16,8,16,128]{3,2,1,0:T(8,128)(2,1)S(1)}, u32[]{:S(2)}) copy-start(bf16[16,8,16,128]{3,2,1,0:T(8,128)(2,1)S(1)} %copy.75) | copy-start | bytes 1572868
  22.9 2.0 %copy-start.9 = (bf16[4,32,2,256]{3,2,1,0:T(2,128)(2,1)S(1)}, bf16[4,32,2,256]{3,2,1,0:T(2,128)(2,1)}, u32[]{:S(2)}) copy-start(bf16[4,32,2,256]{3,2,1,0:T(2,128)(2,1)} %param.11) | copy-start | bytes 393220
  26.2 2.1 %copy-start.5 = (bf16[4,256,1,256]{1,3,0,2:T(8,128)(2,1)}, bf16[4,256,1,256]{1,3,0,2:T(8,128)(2,1)S(1)}, u32[]{:S(2)}) copy-start(bf16[4,256,1,256]{1,3,0,2:T(8,128)(2,1)S(1)} %copy.42) | copy-start | bytes 1572868
  28.3 2.0 %copy-start.2 = (bf16[4,256,1,256]{1,3,0,2:T(8,128)(2,1)S(1)}, bf16[4,256,1,256]{1,3,0,2:T(8,128)(2,1)}, u32[]{:S(2)}) copy-start(bf16[4,256,1,256]{1,3,0,2:T(8,128)(2,1)} %copy.41) | copy-start | bytes 1572868
  30.8 5.0 %copy-start.10 = (f32[2048]{0:T(1024)S(1)}, f32[2048]{0:T(1024)}, u32[]{:S(2)}) copy-start(f32[2048]{0:T(1024)} %param.14) | copy-start | bytes 24580
  32.4 26.6 %copy-start.11 = (s32[32]{0:T(128)S(1)}, s32[32]{0:T(128)}, u32[]{:S(2)}) copy-start(s32[32]{0:T(128)} %param.17) | copy-start | bytes 388
  38.3 23.5 %copy-start.12 = (f32[4]{0:T(128)}, f32[4]{0:T(128)S(1)}, u32[]{:S(2)}) copy-start(f32[4]{0:T(128)S(1)} %psum.7) | copy-start | bytes 52
  61.9 1.2 %copy-start.3 = (bf16[4,256,1,256]{1,3,0,2:T(8,128)(2,1)S(1)}, bf16[4,256,1,256]{1,3,0,2:T(8,128)(2,1)}, u32[]{:S(2)}) copy-start(bf16[4,256,1,256]{1,3,0,2:T(8,128)(2,1)} %copy.41) | copy-start | bytes 1572868
  61.9 1.8 %copy-start.4 = (f32[4,2,8,32,256]{4,3,2,1,0:T(8,128)S(1)}, f32[4,2,8,32,256]{4,3,2,1,0:T(8,128)}, u32[]{:S(2)}) copy-start(f32[4,2,8,32,256]{4,3,2,1,0:T(8,128)} %get-tuple-element.43) | copy-start | bytes 6291460
  71.5 2.6 %copy-start = (bf16[5,224,2,256]{3,0,2,1:T(8,128)(2,1)}, bf16[5,224,2,256]{3,0,2,1:T(8,128)(2,1)S(1)}, u32[]{:S(2)}) copy-start(bf16[5,224,2,256]{3,0,2,1:T(8,128)(2,1)S(1)} %fusion.7) | copy-start | bytes 3440644
  71.5 9.3 %copy-start.6 = (bf16[4,256,1,256]{1,3,0,2:T(8,128)(2,1)S(1)}, bf16[4,256,1,256]{1,3,0,2:T(8,128)(2,1)}, u32[]{:S(2)}) copy-start(bf16[4,256,1,256]{1,3,0,2:T(8,128)(2,1)} %copy-done.5) | copy-start | bytes 1572868
  74.0 15.6 %collective-permute-start.7 = (bf16[1,224,2,256]{3,0,2,1:T(2,128)(2,1)}, bf16[1,224,2,256]{3,0,2,1:T(2,128)(2,1)}, u32[]{:S(2)}, u32[]{:S(2)}) collective-permute-start(bf16[1,224,2,256]{3,0,2,1:T(2,128)(2,1)} %get-tuple-element.35), channel_id=1, source_target_pairs={{12,0},{14,2},{0,4},{2,6},{4,8},{6,10},{8,12},{10,14},{13,1},{15,3... | collective-permute-start | bytes 688136 | tf_op jit(solution)/shard_map/ppermute | solution.py:15
  74.0 26.6 %collective-permute-start.6 = (bf16[1,224,2,256]{3,0,2,1:T(2,128)(2,1)}, bf16[1,224,2,256]{3,0,2,1:T(2,128)(2,1)}, u32[]{:S(2)}, u32[]{:S(2)}) collective-permute-start(bf16[1,224,2,256]{3,0,2,1:T(2,128)(2,1)} %get-tuple-element.36), channel_id=1, source_target_pairs={{14,0},{0,2},{2,4},{4,6},{6,8},{8,10},{10,12},{12,14},{15,1},{1,3}... | collective-permute-start | bytes 688136 | tf_op jit(solution)/shard_map/ppermute | solution.py:15
  75.8 24.8 %collective-permute-start.5 = (bf16[1,224,2,256]{3,0,2,1:T(2,128)(2,1)}, bf16[1,224,2,256]{3,0,2,1:T(2,128)(2,1)}, u32[]{:S(2)}, u32[]{:S(2)}) collective-permute-start(bf16[1,224,2,256]{3,0,2,1:T(2,128)(2,1)} %get-tuple-element.37), channel_id=1, source_target_pairs={{2,0},{4,2},{6,4},{8,6},{10,8},{12,10},{14,12},{0,14},{3,1},{5,3},... | collective-permute-start | bytes 688136 | tf_op jit(solution)/shard_map/ppermute | solution.py:15
  79.1 25.0 %collective-permute-start.4 = (bf16[1,224,2,256]{3,0,2,1:T(2,128)(2,1)}, bf16[1,224,2,256]{3,0,2,1:T(2,128)(2,1)}, u32[]{:S(2)}, u32[]{:S(2)}) collective-permute-start(bf16[1,224,2,256]{3,0,2,1:T(2,128)(2,1)} %get-tuple-element.34), channel_id=1, source_target_pairs={{4,0},{6,2},{8,4},{10,6},{12,8},{14,10},{0,12},{2,14},{5,1},{7,3},... | collective-permute-start | bytes 688136 | tf_op jit(solution)/shard_map/ppermute | solution.py:15
where the time goes:
time: 110 us
  local copies, waits for them, and re-layouts  25 us (23%)
  waiting for transfers between devices  24.3 us (22%)
  blocking collectives  22.2 us (20%)
  starting transfers between devices  14.8 us (13%)
  other arithmetic  10.5 us (10%)
  matrix products  9.5 us (9%)
  between operations  3.43 us (3%)
    ppermute x8, waiting for transfers between devices, passed_along(): return lax.ppermute(block, axis, route)  24.3 us
    unnamed x1, blocking collectives  19.7 us
    ppermute x8, starting transfers between devices, passed_along(): return lax.ppermute(block, axis, route)  14.8 us
    unnamed x41, local copies, waits for them, and re-layouts  9.25 us
    convert_element_type x1, other arithmetic, per_device(): grad_prefix = prefix_total[None].astype(jnp.bfloat16)  3.54 us
    dot_general x1, matrix products, per_device(): jnp.einsum('rm,rlck->mlck', selector, d_rows[:, :prefix_len], precision=l...  2.55 us
    slice x1, local copies, waits for them, and re-layouts, per_device(): arrived = send_home(by_reach[reach_by + SPAN][None], reach_by)  2.54 us
    psum x1, blocking collectives, per_device(): own_rewards = lax.psum(partial_reward, 'tensor')  2.46 us
  transfers between devices with their start and end apart: 8, of which 5 were waited for; matrix products, arithmetic and copies ran while one was open for 9% of the time, Pallas kernels for 0%

commit v1 on v0

v1 whole, which is shorter than its diff:
```python
import functools
import math

import jax
import jax.numpy as jnp
from jax import lax
from jax.experimental import pallas as pl
from jax.experimental.pallas import tpu as pltpu
from jax.sharding import PartitionSpec as P

HD = 128
SPAN = 2
LAST_ROWS = 16
MESH = pl.DeviceIdType.MESH


def dot(a, b, contract_a, contract_b):
    return lax.dot_general(
        a, b, (((contract_a,), (contract_b,)), ((), ())), preferred_element_type=jnp.float32
    )


def kernel(
    n_dp,
    n_tensor,
    offsets,
    queries_hbm,
    upstream_hbm,
    prefix,
    response,
    probe,
    partner,
    labels,
    rewards_out,
    loss_out,
    grad_q_hbm,
    grad_r_out,
    grad_p_out,
    q_buf,
    up_buf,
    gq_buf,
    near0,
    near1,
    near2,
    near3,
    d_rows,
    w_last,
    p_last,
    o_last,
    q_last,
    message,
    table,
    reward_sum,
    out_a,
    out_b,
    out_c,
    out_d,
    in_a,
    in_b,
    in_c,
    in_d,
    local_sem,
    fwd_send,
    fwd_recv,
    bwd_send,
    bwd_recv,
    rew_send,
    rew_recv,
):
    slots, rows, width = q_buf.shape
    chunks, prefix_len, _ = prefix.shape
    heads_kv = chunks // 2
    group = width // HD // heads_kv
    keys = prefix_len + rows
    m_len = group * rows
    near = (near0, near1, near2, near3)
    scale = 1.0 / math.sqrt(HD)

    me = lax.axis_index("dp")
    my_t = lax.axis_index("tensor")
    odd = lax.rem(me, 2)
    mate = me + 1 - 2 * odd
    ahead = lax.rem(me + 2, n_dp)
    behind = lax.rem(me + n_dp - 2, n_dp)
    n_all = n_dp * n_tensor
    my_all = me * n_tensor + my_t

    def place(step):
        other = lax.rem(my_all + step, n_all)
        return {"dp": lax.div(other, n_tensor), "tensor": lax.rem(other, n_tensor)}

    load_q = pltpu.make_async_copy(queries_hbm, q_buf, local_sem.at[0])
    load_up = pltpu.make_async_copy(upstream_hbm, up_buf, local_sem.at[1])
    load_q.start()
    load_up.start()

    barrier = pltpu.get_barrier_semaphore()

    def greet(step, carry):
        pl.semaphore_signal(barrier, inc=1, device_id=place(step), device_id_type=MESH)
        return carry

    lax.fori_loop(1, n_all, greet, 0)
    pl.semaphore_wait(barrier, n_all - 1)

    def forward_copy(chunk, kind):
        if kind == 0:
            src, dst, to = prefix.at[chunk], near[chunk].at[1 + 2 * odd], mate
        elif kind == 1:
            src, dst, to = prefix.at[chunk], near[chunk].at[0], ahead
        elif kind == 2:
            src, dst, to = prefix.at[chunk], near[chunk].at[4], behind
        else:
            src, dst, to = near[chunk].at[4 - 4 * odd], near[chunk].at[3 - 2 * odd], mate
        return pltpu.make_async_remote_copy(
            src_ref=src,
            dst_ref=dst,
            send_sem=fwd_send.at[chunk, kind],
            recv_sem=fwd_recv.at[chunk, kind],
            device_id={"dp": to},
            device_id_type=MESH,
        )

    fwd = [[forward_copy(c, k) for k in range(4)] for c in range(chunks)]
    for c in range(chunks):
        for k in (1, 2, 0):
            fwd[c][k].start()

    lane = lax.broadcasted_iota(jnp.int32, (1, m_len), 1)
    token = lax.rem(lane, rows)
    not_last = jnp.where(token == rows - 1, 0.0, 1.0)
    causal = lax.broadcasted_iota(jnp.int32, (rows, m_len), 0) <= lax.rem(
        lax.broadcasted_iota(jnp.int32, (rows, m_len), 1), rows
    )
    pick = jnp.where(
        lax.broadcasted_iota(jnp.int32, (LAST_ROWS, m_len), 0) * rows + (rows - 1)
        == lax.broadcasted_iota(jnp.int32, (LAST_ROWS, m_len), 1),
        1.0,
        0.0,
    ).astype(jnp.bfloat16)

    def stacked(buf, r, g):
        return jnp.concatenate(
            [buf[r, :, (g * group + h) * HD : (g * group + h + 1) * HD] for h in range(group)],
            axis=0,
        )

    def key_value(r, g, prefix_k, prefix_v):
        mine = pl.ds(pl.multiple_of(r * rows, rows), rows)
        return (
            jnp.concatenate([prefix_k, response[2 * g, mine]], axis=0),
            jnp.concatenate([prefix_v, response[2 * g + 1, mine]], axis=0),
        )

    def probe_of(g):
        return jnp.concatenate(
            [probe[g * group : (g + 1) * group], jnp.zeros((LAST_ROWS - group, HD), jnp.float32)],
            axis=0,
        )

    def last_token(r, g, k, v):
        q31 = dot(pick, stacked(q_buf, r, g), 1, 0).astype(jnp.bfloat16)
        s = dot(q31, k, 1, 1)
        e = jnp.exp((s - jnp.max(s, axis=1, keepdims=True)) * scale)
        w = e / jnp.sum(e, axis=1, keepdims=True)
        w_low = w.astype(jnp.bfloat16)
        o = dot(w_low, v, 1, 0)
        q_last[r, g] = q31
        w_last[r, g] = w_low
        p_last[r, g] = w
        o_last[r, g] = o
        return jnp.sum(
            jnp.sum(o * probe_of(g), axis=0, keepdims=True), axis=1, keepdims=True
        )

    def main(r, g, k, v):
        q = stacked(q_buf, r, g)
        d_out = stacked(up_buf, r, g)
        s = dot(k, q, 1, 1)
        s = jnp.concatenate(
            [s[:prefix_len], jnp.where(causal, s[prefix_len:], -1e30)], axis=0
        )
        e = jnp.exp((s - jnp.max(s, axis=0, keepdims=True)) * scale)
        w = e * (not_last / jnp.sum(e, axis=0, keepdims=True))
        w_low = w.astype(jnp.bfloat16)
        dw = dot(v, d_out, 1, 1)
        delta = jnp.sum(w_low.astype(jnp.float32) * dw, axis=0, keepdims=True)
        ds = (w * (dw - delta) * scale).astype(jnp.bfloat16)
        d_rows[r, 2 * g] = dot(ds, q, 1, 0)
        d_rows[r, 2 * g + 1] = dot(w_low, d_out, 1, 0)
        dq = dot(ds, k, 0, 0).astype(jnp.bfloat16)
        for h in range(group):
            gq_buf[r, :, (g * group + h) * HD : (g * group + h + 1) * HD] = dq[
                h * rows : (h + 1) * rows
            ]

    slot_row = lax.broadcasted_iota(jnp.int32, (8, HD), 0)

    load_q.wait()
    load_up.wait()

    def near_slot(r, note):
        for g in range(heads_kv):
            k, v = key_value(r, g, prefix[2 * g], prefix[2 * g + 1])
            note = note + jnp.where(slot_row == r, last_token(r, g, k, v), 0.0)
            main(r, g, k, v)
        return note

    note = lax.fori_loop(0, 2, near_slot, jnp.zeros((8, HD), jnp.float32))
    for c in range(chunks):
        near[c][2] = prefix[c]

    for c in range(chunks):
        kind = 2 - odd
        pltpu.make_async_remote_copy(
            src_ref=prefix.at[c],
            dst_ref=near[c].at[4 - 4 * odd],
            send_sem=fwd_send.at[c, kind],
            recv_sem=fwd_recv.at[c, kind],
            device_id={"dp": mate},
            device_id_type=MESH,
        ).wait_recv()
        fwd[c][3].start()
    for c in range(chunks):
        kind = 1 + odd
        pltpu.make_async_remote_copy(
            src_ref=prefix.at[c],
            dst_ref=near[c].at[4 * odd],
            send_sem=fwd_send.at[c, kind],
            recv_sem=fwd_recv.at[c, kind],
            device_id={"dp": mate},
            device_id_type=MESH,
        ).wait_recv()
        fwd[c][0].wait_recv()
        fwd[c][3].wait_recv()

    def far_keys(r, g):
        reach = offsets[0, r] + SPAN
        return key_value(r, g, near[2 * g][reach], near[2 * g + 1][reach])

    def far_reward(r, note):
        for g in range(heads_kv):
            k, v = far_keys(r, g)
            note = note + jnp.where(slot_row == r, last_token(r, g, k, v), 0.0)
        return note

    note = lax.fori_loop(2, slots, far_reward, note)
    message[...] = note
    table[my_all] = note

    def reward_copy(step):
        return pltpu.make_async_remote_copy(
            src_ref=message,
            dst_ref=table.at[my_all],
            send_sem=rew_send.at[step],
            recv_sem=rew_recv.at[step],
            device_id=place(step),
            device_id_type=MESH,
        )

    def tell(step, carry):
        reward_copy(step).start()
        return carry

    lax.fori_loop(1, n_all, tell, 0)

    def far_slot(r, carry):
        for g in range(heads_kv):
            k, v = far_keys(r, g)
            main(r, g, k, v)
        return carry

    lax.fori_loop(2, slots, far_slot, 0)

    def hear(step, carry):
        reward_copy(step).wait()
        return carry

    lax.fori_loop(1, n_all, hear, 0)

    summed = jnp.sum(table[...].reshape(n_dp, n_tensor, 8, HD), axis=1).reshape(n_dp * 8, HD)
    reward_sum[...] = summed
    resp = partner.shape[1]
    other = partner[...]
    label = labels[...]
    all_rows = lax.broadcasted_iota(jnp.int32, (n_dp * 8, resp), 0)
    all_ids = lax.rem(all_rows, 8) + lax.div(all_rows, 8) * slots
    all_ids = jnp.where(lax.rem(all_rows, 8) < slots, all_ids, -1)
    pair = lax.broadcasted_iota(jnp.int32, (n_dp * 8, resp), 1)
    column = summed[:, :1]
    first = jnp.sum(jnp.where(all_ids == pair, column, 0.0), axis=0, keepdims=True)
    second = jnp.sum(jnp.where(all_ids == other, column, 0.0), axis=0, keepdims=True)
    middle = 0.5 * (first + second)
    exp_first = jnp.exp(first)
    exp_second = jnp.exp(second)
    exp_middle = jnp.exp(middle)
    totals = exp_first + exp_second + exp_middle
    chosen = jnp.where(label == 0, first, jnp.where(label == 1, second, middle))
    loss = jnp.sum(jnp.log(totals) - chosen, axis=1, keepdims=True) * (1.0 / resp)
    loss_out[0] = loss[0, 0]
    tie_share = 0.5 * exp_middle / totals
    half_tie = jnp.where(label == 2, 0.5, 0.0)
    grad_first = exp_first / totals + tie_share - jnp.where(label == 0, 1.0, 0.0) - half_tie
    grad_second = exp_second / totals + tie_share - jnp.where(label == 1, 1.0, 0.0) - half_tie
    my_rows = lax.broadcasted_iota(jnp.int32, (8, resp), 0)
    my_ids = jnp.where(my_rows < slots, my_rows + me * slots, -1)
    my_pair = lax.broadcasted_iota(jnp.int32, (8, resp), 1)
    grads = jnp.sum(
        jnp.where(my_ids == my_pair, grad_first, 0.0) + jnp.where(my_ids == other, grad_second, 0.0),
        axis=1,
        keepdims=True,
    )
    own = reward_sum[pl.ds(pl.multiple_of(me * 8, 8), 8)]
    for j in range(slots):
        rewards_out[j] = own[j, 0]

    def finish(r, g, k, v):
        mine = jnp.sum(
            jnp.where(slot_row[:, :1] == r, grads, 0.0), axis=0, keepdims=True
        )
        up31 = dot(pick, stacked(up_buf, r, g), 1, 0)
        d31 = (up31 + mine * probe_of(g)).astype(jnp.bfloat16)
        dw = dot(d31, v, 1, 1)
        delta = jnp.sum(d31.astype(jnp.float32) * o_last[r, g], axis=1, keepdims=True)
        ds = (p_last[r, g] * (dw - delta) * scale).astype(jnp.bfloat16)
        dk = d_rows[r, 2 * g] + dot(ds, q_last[r, g], 0, 0)
        dv = d_rows[r, 2 * g + 1] + dot(w_last[r, g], d31, 0, 0)
        dq = dot(pick, dot(ds, k, 1, 0).astype(jnp.bfloat16), 0, 0).astype(jnp.bfloat16)
        for h in range(group):
            cols = slice((g * group + h) * HD, (g * group + h + 1) * HD)
            gq_buf[r, :, cols] = gq_buf[r, :, cols] + dq[h * rows : (h + 1) * rows]
        mine_rows = pl.ds(pl.multiple_of(r * rows, rows), rows)
        grad_r_out[2 * g, mine_rows] = dk[prefix_len:].astype(jnp.bfloat16)
        grad_r_out[2 * g + 1, mine_rows] = dv[prefix_len:].astype(jnp.bfloat16)
        return dk[:prefix_len], dv[:prefix_len]

    def backward_copy(chunk, kind):
        src = (out_a, out_b, out_c, out_d)[kind].at[chunk]
        dst = (in_a, in_b, in_c, in_d)[kind].at[chunk]
        if kind < 2:
            to = mate
        elif kind == 2:
            to = lax.rem(me + n_dp + 4 * odd - 2, n_dp)
        else:
            to = lax.rem(me + n_dp + 2 - 4 * odd, n_dp)
        return pltpu.make_async_remote_copy(
            src_ref=src,
            dst_ref=dst,
            send_sem=bwd_send.at[chunk, kind],
            recv_sem=bwd_recv.at[chunk, kind],
            device_id={"dp": to},
            device_id_type=MESH,
        )

    bwd = [[backward_copy(c, k) for k in range(4)] for c in range(chunks)]
    reach2 = offsets[0, 2]
    reach3 = offsets[0, 3]

    def part(d2, d3, reach):
        return jnp.where(reach2 == reach, d2, 0.0) + jnp.where(reach3 == reach, d3, 0.0)

    for g in range(heads_kv):
        pairs = [finish(r, g, *far_keys(r, g)) for r in (2, 3)]
        for c in range(2):
            chunk = 2 * g + c
            d2, d3 = pairs[0][c], pairs[1][c]
            out_a[chunk] = part(d2, d3, 2 * odd - 1).astype(jnp.bfloat16)
            bwd[chunk][0].start()
            out_c[chunk] = part(d2, d3, 4 * odd - 2).astype(jnp.bfloat16)
            bwd[chunk][2].start()
            out_b[chunk] = part(d2, d3, 1 - 2 * odd).astype(jnp.bfloat16)
            bwd[chunk][1].start()
            d_rows[2, chunk, :prefix_len] = part(d2, d3, 0)
            d_rows[3, chunk, :prefix_len] = part(d2, d3, 2 - 4 * odd)

    for c in range(chunks):
        bwd[c][0].wait_recv()
        out_d[c] = (
            d_rows[3, c, :prefix_len] + in_a[c].astype(jnp.float32)
        ).astype(jnp.bfloat16)
        bwd[c][3].start()

    for g in range(heads_kv):
        for r in (0, 1):
            k, v = key_value(r, g, prefix[2 * g], prefix[2 * g + 1])
            dk, dv = finish(r, g, k, v)
            d_rows[2, 2 * g, :prefix_len] += dk
            d_rows[2, 2 * g + 1, :prefix_len] += dv
    store_q = pltpu.make_async_copy(gq_buf, grad_q_hbm, local_sem.at[2])
    store_q.start()

    for c in range(chunks):
        bwd[c][1].wait_recv()
        bwd[c][2].wait_recv()
        bwd[c][3].wait_recv()
        grad_p_out[c] = (
            d_rows[2, c, :prefix_len]
            + in_b[c].astype(jnp.float32)
            + in_c[c].astype(jnp.float32)
            + in_d[c].astype(jnp.float32)
        ).astype(jnp.bfloat16)

    for c in range(chunks):
        for k in range(4):
            fwd[c][k].wait_send()
            bwd[c][k].wait_send()
    store_q.wait()


def per_device(
    n_dp,
    n_tensor,
    queries,
    response_cache,
    prefix_cache,
    upstream,
    reward_probe,
    slot_offsets,
    partner,
    labels,
):
    slots, rows, width = queries.shape
    prefix_len = prefix_cache.shape[1]
    kv_heads = response_cache.shape[3] // HD
    chunks = 2 * kv_heads
    keys = prefix_len + rows
    resp = partner.shape[0]
    n_all = n_dp * n_tensor
    prefix = prefix_cache.reshape(prefix_len, 2, kv_heads, HD).transpose(2, 1, 0, 3)
    prefix = prefix.reshape(chunks, prefix_len, HD)
    response = response_cache.reshape(slots * rows, 2, kv_heads, HD).transpose(2, 1, 0, 3)
    response = response.reshape(chunks, slots * rows, HD)
    vmem = pl.BlockSpec(memory_space=pltpu.VMEM)
    smem = pl.BlockSpec(memory_space=pltpu.SMEM)
    hbm = pl.BlockSpec(memory_space=pl.ANY)
    near = pltpu.VMEM((2 * SPAN + 1, prefix_len, HD), jnp.bfloat16)
    block = pltpu.VMEM((chunks, prefix_len, HD), jnp.bfloat16)
    rewards, loss, grad_q, grad_r, grad_p = pl.pallas_call(
        functools.partial(kernel, n_dp, n_tensor),
        out_shape=(
            jax.ShapeDtypeStruct((slots,), jnp.float32),
            jax.ShapeDtypeStruct((1,), jnp.float32),
            jax.ShapeDtypeStruct(queries.shape, jnp.bfloat16),
            jax.ShapeDtypeStruct((chunks, slots * rows, HD), jnp.bfloat16),
            jax.ShapeDtypeStruct((chunks, prefix_len, HD), jnp.bfloat16),
        ),
        in_specs=[smem, hbm, hbm, vmem, vmem, vmem, vmem, vmem],
        out_specs=(smem, smem, hbm, vmem, vmem),
        scratch_shapes=[
            pltpu.VMEM(queries.shape, jnp.bfloat16),
            pltpu.VMEM(queries.shape, jnp.bfloat16),
            pltpu.VMEM(queries.shape, jnp.bfloat16),
            near,
            near,
            near,
            near,
            pltpu.VMEM((slots, chunks, keys, HD), jnp.float32),
            pltpu.VMEM((slots, kv_heads, LAST_ROWS, keys), jnp.bfloat16),
            pltpu.VMEM((slots, kv_heads, LAST_ROWS, keys), jnp.float32),
            pltpu.VMEM((slots, kv_heads, LAST_ROWS, HD), jnp.float32),
            pltpu.VMEM((slots, kv_heads, LAST_ROWS, HD), jnp.bfloat16),
            pltpu.VMEM((8, HD), jnp.float32),
            pltpu.VMEM((n_all, 8, HD), jnp.float32),
            pltpu.VMEM((n_dp * 8, HD), jnp.float32),
            block,
            block,
            block,
            block,
            block,
            block,
            block,
            block,
            pltpu.SemaphoreType.DMA((3,)),
            pltpu.SemaphoreType.DMA((chunks, 4)),
            pltpu.SemaphoreType.DMA((chunks, 4)),
            pltpu.SemaphoreType.DMA((chunks, 4)),
            pltpu.SemaphoreType.DMA((chunks, 4)),
            pltpu.SemaphoreType.DMA((n_all,)),
            pltpu.SemaphoreType.DMA((n_all,)),
        ],
        compiler_params=pltpu.CompilerParams(
            collective_id=0, has_side_effects=True, vmem_limit_bytes=40 * 1024 * 1024
        ),
    )(
        slot_offsets,
        queries,
        upstream,
        prefix,
        response,
        reward_probe.reshape(width // HD, HD),
        partner.reshape(1, resp),
        labels.reshape(1, resp),
    )
    grad_response = grad_r.reshape(kv_heads, 2, slots, rows, HD).transpose(2, 3, 1, 0, 4)
    grad_prefix = grad_p.reshape(kv_heads, 2, 1, prefix_len, HD).transpose(2, 3, 1, 0, 4)
    return (
        rewards,
        loss,
        grad_q,
        grad_response.reshape(response_cache.shape),
        grad_prefix.reshape(prefix_cache.shape),
    )


def solution(mesh):
    in_specs = (
        P(("group", "dp"), None, "tensor"),
        P(("group", "dp"), None, None, "tensor"),
        P(("group", "dp"), None, None, "tensor"),
        P(("group", "dp"), None, "tensor"),
        P("tensor"),
        P(("group", "dp"), None),
        P("group"),
        P("group"),
    )
    out_specs = (
        P(("group", "dp")),
        P("group"),
        P(("group", "dp"), None, "tensor"),
        P(("group", "dp"), None, None, "tensor"),
        P(("group", "dp"), None, None, "tensor"),
    )
    return jax.shard_map(
        functools.partial(per_device, mesh.shape["dp"], mesh.shape["tensor"]),
        mesh=mesh,
        in_specs=in_specs,
        out_specs=out_specs,
        check_vma=False,
    )
```

time: 110 us -> 53.2 us (0.48)
  Pallas kernels: 0 us -> 45.2 us
  waiting for transfers between devices: 24.3 us -> 0 us
  blocking collectives: 22.2 us -> 0 us
  local copies, waits for them, and re-layouts: 25 us -> 5.44 us
  starting transfers between devices: 14.8 us -> 0 us
  other arithmetic: 10.5 us -> 0 us
  matrix products: 9.5 us -> 0 us
    pallas_call x0 -> x1, Pallas kernels: none -> 45.2 us  [per_device(): pl.pallas_call(functools.partial(kernel, n_dp, n_tensor), out_shape=(jax....]
    ppermute x8 -> x0, waiting for transfers between devices: 24.3 us -> none  [passed_along(): return lax.ppermute(block, axis, route)]
    unnamed x1 -> x0, blocking collectives: 19.7 us -> none
    ppermute x8 -> x0, starting transfers between devices: 14.8 us -> none  [passed_along(): return lax.ppermute(block, axis, route)]
    dot_general x6 -> x0, matrix products: 7.42 us -> none  [the longest x1 2.55 us: per_device(): jnp.einsum('rm,rlck->mlck', selector, d_rows[:, :prefix_len], precision=l...]
    unnamed x41 -> x16, local copies, waits for them, and re-layouts: 9.25 us -> 2.25 us
    convert_element_type x4 -> x0, other arithmetic: 5.69 us -> none  [the longest x1 3.54 us: per_device(): grad_prefix = prefix_total[None].astype(jnp.bfloat16)]
    slice x5 -> x0, local copies, waits for them, and re-layouts: 4.8 us -> none  [the longest x1 2.54 us: per_device(): arrived = send_home(by_reach[reach_by + SPAN][None], reach_by)]
  transfers between devices with their start and end apart: 8 -> 0, of which waited for: 5 -> 0; matrix products, arithmetic and copies ran while one was open for 9% -> 0% of each run, Pallas kernels for 0% -> 0%
where the time goes in v1:
time: 53.2 us; the launch traced here: 53.1 us
  Pallas kernels  45.2 us (85%)
  local copies, waits for them, and re-layouts  5.44 us (10%)
  between operations  2.44 us (5%)
    pallas_call x1, Pallas kernels, per_device(): pl.pallas_call(functools.partial(kernel, n_dp, n_tensor), out_shape=(jax....  45.2 us
    unnamed x16, local copies, waits for them, and re-layouts  2.25 us

profile of v1, /device:TPU:0, one launch (start us, length us, event | category | flops | bytes accessed | tf_op | source)
XLA Modules:
  0.0 53.1 jit_solution(2237470146295047547)
XLA Ops:
  0.6 0.0 copy-start.6
  0.6 1.0 %reshape.45 = bf16[128,2,2,128]{3,2,1,0:T(2,128)(2,1)S(1)} reshape(bf16[4,32,2,256]{3,2,1,0:T(2,128)(2,1)} %param.9) | data formatting | bytes 262144 | tf_op jit(solution)/shard_map/reshape | solution.py:431
  1.7 0.0 copy-start.1
  1.7 0.0 copy-start
  1.7 0.0 copy-done.6
  1.7 0.1 reshape.43
  1.9 0.0 copy-start.2
  1.9 0.0 copy-start.3
  2.0 0.0 copy-start.4
  2.0 0.0 copy-start.5
  2.0 0.7 %copy-done.1 = bf16[4,32,2048]{2,1,0:T(8,128)(2,1)S(1)} copy-done((bf16[4,32,2048]{2,1,0:T(8,128)(2,1)S(1)}, bf16[4,32,2048]{2,1,0:T(8,128)(2,1)}, u32[]{:S(2)}) %copy-start.1) | copy-done | bytes 524312
  2.7 0.2 copy-done
  2.9 0.0 copy-done.2
  2.9 0.0 copy-done.3
  2.9 0.0 copy-done.4
  2.9 0.0 copy-done.5
  2.9 45.2 %shard_map.119 = (f32[4]{0:T(128)S(1)}, f32[1]{0:T(128)}, bf16[4,32,2048]{2,1,0:T(8,128)(2,1)S(1)}, bf16[4,128,128]{2,1,0:T(8,128)(2,1)S(1)}, bf16[4,224,128]{2,1,0:T(8,128)(2,1)S(1)}) custom-call(s32[1,4]{1,0:T(1,128)S(1)} %copy-done.3, bf16[4,32,2048]{2,1,0:T(8,128)(2,1)S(1)} %copy-done, bf16[4,32,2048]{2,1,0:T(8,128)(2,1)S(1)} %copy-done.1, ...), custom_call_target="tpu_custom_call" | custom-call | tf_op jit(solution)/shard_map/pallas_call | solution.py:438
  48.1 0.1 copy.15
  48.2 0.7 %reshape.51 = bf16[4,32,2,256]{3,2,1,0:T(2,128)(2,1)} reshape(bf16[4,32,2,2,128]{4,3,2,1,0:T(2,128)(2,1)S(1)} %copy.15) | data formatting | bytes 262144 | tf_op jit(solution)/shard_map/reshape | solution.py:500
  49.0 0.2 copy.16
  49.2 0.8 %reshape.53 = bf16[1,224,2,256]{3,2,1,0:T(2,128)(2,1)} reshape(bf16[1,224,2,2,128]{4,3,2,1,0:T(2,128)(2,1)S(1)} %copy.16) | data formatting | bytes 458752 | tf_op jit(solution)/shard_map/reshape | solution.py:501
  50.1 0.5 copy.20
  51.1 0.8 %copy.22 = bf16[4,32,2048]{2,1,0:T(8,128)(2,1)} copy(bf16[4,32,2048]{2,1,0:T(8,128)(2,1)S(1)} %get-tuple-element.22) | data formatting | bytes 1048576
  (2 shorter events, 0.1 us)
Async XLA Ops:
  0.6 1.1 %copy-start.6 = (bf16[1,224,2,256]{3,2,1,0:T(2,128)(2,1)S(1)}, bf16[1,224,2,256]{3,2,1,0:T(2,128)(2,1)}, u32[]{:S(2)}) copy-start(bf16[1,224,2,256]{3,2,1,0:T(2,128)(2,1)} %param.10) | copy-start | bytes 688132
  1.7 1.0 %copy-start.1 = (bf16[4,32,2048]{2,1,0:T(8,128)(2,1)S(1)}, bf16[4,32,2048]{2,1,0:T(8,128)(2,1)}, u32[]{:S(2)}) copy-start(bf16[4,32,2048]{2,1,0:T(8,128)(2,1)} %upstream_hbm.1) | copy-start | bytes 1572868
  1.7 1.2 %copy-start = (bf16[4,32,2048]{2,1,0:T(8,128)(2,1)S(1)}, bf16[4,32,2048]{2,1,0:T(8,128)(2,1)}, u32[]{:S(2)}) copy-start(bf16[4,32,2048]{2,1,0:T(8,128)(2,1)} %queries_hbm.1) | copy-start | bytes 1572868
  1.9 1.0 %copy-start.2 = (f32[2048]{0:T(1024)S(1)}, f32[2048]{0:T(1024)}, u32[]{:S(2)}) copy-start(f32[2048]{0:T(1024)} %param.12) | copy-start | bytes 24580
  1.9 0.9 %copy-start.3 = (s32[1,4]{1,0:T(1,128)S(1)}, s32[1,4]{1,0:T(1,128)}, u32[]{:S(2)}) copy-start(s32[1,4]{1,0:T(1,128)} %offsets.1) | copy-start | bytes 52
  2.0 0.9 %copy-start.4 = (s32[32]{0:T(128)S(1)}, s32[32]{0:T(128)}, u32[]{:S(2)}) copy-start(s32[32]{0:T(128)} %param.14) | copy-start | bytes 388
  2.0 0.9 %copy-start.5 = (s32[32]{0:T(128)S(1)}, s32[32]{0:T(128)}, u32[]{:S(2)}) copy-start(s32[32]{0:T(128)} %param.15) | copy-start | bytes 388

commit v2 on v1

--- a/solution.py
+++ b/solution.py
@@ -51,6 +51,11 @@
     message,
     table,
     reward_sum,
+    sent_rows,
+    got_rows,
+    sent_stats,
+    got_stats,
+    stats_near,
     out_a,
     out_b,
     out_c,
@@ -66,10 +71,13 @@
     bwd_recv,
     rew_send,
     rew_recv,
+    note_send,
+    note_recv,
 ):
     slots, rows, width = q_buf.shape
-    chunks, prefix_len, _ = prefix.shape
-    heads_kv = chunks // 2
+    _, prefix_len, kv_width = prefix.shape
+    heads_kv = kv_width // HD
+    chunks = 2 * heads_kv
     group = width // HD // heads_kv
     keys = prefix_len + rows
     m_len = group * rows
@@ -103,13 +111,19 @@
     lax.fori_loop(1, n_all, greet, 0)
     pl.semaphore_wait(barrier, n_all - 1)
 
+    def head(g):
+        return slice(g * HD, (g + 1) * HD)
+
+    def prefix_at(chunk):
+        return prefix.at[chunk % 2, :, head(chunk // 2)]
+
     def forward_copy(chunk, kind):
         if kind == 0:
-            src, dst, to = prefix.at[chunk], near[chunk].at[1 + 2 * odd], mate
+            src, dst, to = prefix_at(chunk), near[chunk].at[1 + 2 * odd], mate
         elif kind == 1:
-            src, dst, to = prefix.at[chunk], near[chunk].at[0], ahead
+            src, dst, to = prefix_at(chunk), near[chunk].at[0], ahead
         elif kind == 2:
-            src, dst, to = prefix.at[chunk], near[chunk].at[4], behind
+            src, dst, to = prefix_at(chunk), near[chunk].at[4], behind
         else:
             src, dst, to = near[chunk].at[4 - 4 * odd], near[chunk].at[3 - 2 * odd], mate
         return pltpu.make_async_remote_copy(
@@ -148,8 +162,8 @@
     def key_value(r, g, prefix_k, prefix_v):
         mine = pl.ds(pl.multiple_of(r * rows, rows), rows)
         return (
-            jnp.concatenate([prefix_k, response[2 * g, mine]], axis=0),
-            jnp.concatenate([prefix_v, response[2 * g + 1, mine]], axis=0),
+            jnp.concatenate([prefix_k, response[0, mine, head(g)]], axis=0),
+            jnp.concatenate([prefix_v, response[1, mine, head(g)]], axis=0),
         )
 
     def probe_of(g):
@@ -169,9 +183,17 @@
         w_last[r, g] = w_low
         p_last[r, g] = w
         o_last[r, g] = o
-        return jnp.sum(
-            jnp.sum(o * probe_of(g), axis=0, keepdims=True), axis=1, keepdims=True
-        )
+        by_head = jnp.sum(o * probe_of(g), axis=1, keepdims=True)
+        stats = [
+            jnp.max(s, axis=1, keepdims=True),
+            1.0 / jnp.sum(e, axis=1, keepdims=True),
+            jnp.sum(o * dot(pick, stacked(up_buf, r, g), 1, 0), axis=1, keepdims=True),
+            by_head,
+        ]
+        packed = jnp.zeros((LAST_ROWS, HD), jnp.float32)
+        for i, stat in enumerate(stats):
+            packed = packed + jnp.where(lane_of == g * len(stats) + i, stat, 0.0)
+        return jnp.sum(by_head, axis=0, keepdims=True), packed
 
     def main(r, g, k, v):
         q = stacked(q_buf, r, g)
@@ -195,58 +217,98 @@
             ]
 
     slot_row = lax.broadcasted_iota(jnp.int32, (8, HD), 0)
+    lane_of = lax.broadcasted_iota(jnp.int32, (LAST_ROWS, HD), 1)
 
     load_q.wait()
     load_up.wait()
 
-    def near_slot(r, note):
+    for g in range(heads_kv):
+        for i, buf in enumerate((q_buf, up_buf)):
+            both = [dot(pick, stacked(buf, r, g), 1, 0)[:group] for r in (2, 3)]
+            sent_rows[i, g] = jnp.concatenate(both, axis=0).astype(jnp.bfloat16)
+
+    def note_copy(which, to):
+        src = (sent_rows, sent_stats)[which]
+        dst = (got_rows, got_stats)[which].at[to]
+        near_by = (1, n_dp - 1, 2, n_dp - 2)[to]
+        return pltpu.make_async_remote_copy(
+            src_ref=src,
+            dst_ref=dst,
+            send_sem=note_send.at[which, to],
+            recv_sem=note_recv.at[which, to],
+            device_id={"dp": lax.rem(me + near_by, n_dp)},
+            device_id_type=MESH,
+        )
+
+    notes = [[note_copy(which, to) for to in range(4)] for which in range(2)]
+
+    note = jnp.zeros((8, HD), jnp.float32)
+    own_stats = []
+    for r in (0, 1):
+        mine = jnp.zeros((LAST_ROWS, HD), jnp.float32)
         for g in range(heads_kv):
-            k, v = key_value(r, g, prefix[2 * g], prefix[2 * g + 1])
-            note = note + jnp.where(slot_row == r, last_token(r, g, k, v), 0.0)
+            k, v = key_value(r, g, prefix[0, :, head(g)], prefix[1, :, head(g)])
+            reward, packed = last_token(r, g, k, v)
+            note = note + jnp.where(slot_row == r, reward, 0.0)
+            mine = mine + packed
             main(r, g, k, v)
-        return note
-
-    note = lax.fori_loop(0, 2, near_slot, jnp.zeros((8, HD), jnp.float32))
-    for c in range(chunks):
-        near[c][2] = prefix[c]
-
-    for c in range(chunks):
-        kind = 2 - odd
+        own_stats.append(mine[:group])
+        if r == 0:
+            for c in range(chunks):
+                near[c][2] = prefix[c % 2, :, head(c // 2)]
+    stats_near[...] = jnp.concatenate(own_stats, axis=0)
+
+    def wait_arrival(c, kind, index):
         pltpu.make_async_remote_copy(
-            src_ref=prefix.at[c],
-            dst_ref=near[c].at[4 - 4 * odd],
+            src_ref=prefix_at(c),
+            dst_ref=near[c].at[index],
             send_sem=fwd_send.at[c, kind],
             recv_sem=fwd_recv.at[c, kind],
             device_id={"dp": mate},
             device_id_type=MESH,
         ).wait_recv()
+
+    for c in range(chunks):
+        wait_arrival(c, 2 - odd, 4 - 4 * odd)
         fwd[c][3].start()
-    for c in range(chunks):
-        kind = 1 + odd
-        pltpu.make_async_remote_copy(
-            src_ref=prefix.at[c],
-            dst_ref=near[c].at[4 * odd],
-            send_sem=fwd_send.at[c, kind],
-            recv_sem=fwd_recv.at[c, kind],
-            device_id={"dp": mate},
+    for to in range(4):
+        notes[0][to].start()
+
+    def backward_copy(chunk, kind):
+        src = (out_a, out_b, out_c, out_d)[kind].at[chunk]
+        dst = (in_a, in_b, in_c, in_d)[kind].at[chunk]
+        if kind < 2:
+            to = mate
+        elif kind == 2:
+            to = lax.rem(me + n_dp + 4 * odd - 2, n_dp)
+        else:
+            to = lax.rem(me + n_dp + 2 - 4 * odd, n_dp)
+        return pltpu.make_async_remote_copy(
+            src_ref=src,
+            dst_ref=dst,
+            send_sem=bwd_send.at[chunk, kind],
+            recv_sem=bwd_recv.at[chunk, kind],
+            device_id={"dp": to},
             device_id_type=MESH,
-        ).wait_recv()
-        fwd[c][0].wait_recv()
-        fwd[c][3].wait_recv()
+        )
+
+    bwd = [[backward_copy(c, k) for k in range(4)] for c in range(chunks)]
+    reach2 = offsets[0, 2]
+    reach3 = offsets[0, 3]
 
     def far_keys(r, g):
         reach = offsets[0, r] + SPAN
         return key_value(r, g, near[2 * g][reach], near[2 * g + 1][reach])
 
-    def far_reward(r, note):
-        for g in range(heads_kv):
-            k, v = far_keys(r, g)
-            note = note + jnp.where(slot_row == r, last_token(r, g, k, v), 0.0)
-        return note
-
-    note = lax.fori_loop(2, slots, far_reward, note)
-    message[...] = note
-    table[my_all] = note
+    def part(d2, d3, reach):
+        return jnp.where(reach2 == reach, d2, 0.0) + jnp.where(reach3 == reach, d3, 0.0)
+
+    def pass_on(c):
+        bwd[c][0].wait_recv()
+        out_d[c] = (
+            d_rows[3, c, :prefix_len] + in_a[c].astype(jnp.float32)
+        ).astype(jnp.bfloat16)
+        bwd[c][3].start()
 
     def reward_copy(step):
         return pltpu.make_async_remote_copy(
@@ -262,15 +324,46 @@
         reward_copy(step).start()
         return carry
 
-    lax.fori_loop(1, n_all, tell, 0)
-
-    def far_slot(r, carry):
-        for g in range(heads_kv):
+    far_stats = [jnp.zeros((LAST_ROWS, HD), jnp.float32)] * 2
+    for g in range(heads_kv):
+        for c in (2 * g, 2 * g + 1):
+            wait_arrival(c, 1 + odd, 4 * odd)
+            fwd[c][0].wait_recv()
+            fwd[c][3].wait_recv()
+        for r in (2, 3):
             k, v = far_keys(r, g)
-            main(r, g, k, v)
-        return carry
-
-    lax.fori_loop(2, slots, far_slot, 0)
+            reward, packed = last_token(r, g, k, v)
+            note = note + jnp.where(slot_row == r, reward, 0.0)
+            far_stats[r - 2] = far_stats[r - 2] + packed
+        if g == heads_kv - 1:
+            for r in (2, 3):
+                note = note + jnp.where(
+                    slot_row == slots + r - 2, offsets[0, r].astype(jnp.float32), 0.0
+                )
+            message[...] = note
+            table[my_all] = note
+            lax.fori_loop(1, n_all, tell, 0)
+            sent_stats[...] = jnp.concatenate([x[:group] for x in far_stats], axis=0)
+            for to in range(4):
+                notes[1][to].start()
+        for r in (2, 3):
+            main(r, g, *far_keys(r, g))
+        for chunk in (2 * g, 2 * g + 1):
+            d2 = d_rows[2, chunk, :prefix_len]
+            d3 = d_rows[3, chunk, :prefix_len]
+            out_a[chunk] = part(d2, d3, 2 * odd - 1).astype(jnp.bfloat16)
+            bwd[chunk][0].start()
+            out_c[chunk] = part(d2, d3, 4 * odd - 2).astype(jnp.bfloat16)
+            bwd[chunk][2].start()
+            out_b[chunk] = part(d2, d3, 1 - 2 * odd).astype(jnp.bfloat16)
+            bwd[chunk][1].start()
+            d_rows[2, chunk, :prefix_len] = part(d2, d3, 0)
+            d_rows[3, chunk, :prefix_len] = part(d2, d3, 2 - 4 * odd)
+        if g > 0:
+            pass_on(2 * g - 2)
+            pass_on(2 * g - 1)
+    pass_on(chunks - 2)
+    pass_on(chunks - 1)
 
     def hear(step, carry):
         reward_copy(step).wait()
@@ -302,98 +395,105 @@
     half_tie = jnp.where(label == 2, 0.5, 0.0)
     grad_first = exp_first / totals + tie_share - jnp.where(label == 0, 1.0, 0.0) - half_tie
     grad_second = exp_second / totals + tie_share - jnp.where(label == 1, 1.0, 0.0) - half_tie
-    my_rows = lax.broadcasted_iota(jnp.int32, (8, resp), 0)
-    my_ids = jnp.where(my_rows < slots, my_rows + me * slots, -1)
-    my_pair = lax.broadcasted_iota(jnp.int32, (8, resp), 1)
-    grads = jnp.sum(
-        jnp.where(my_ids == my_pair, grad_first, 0.0) + jnp.where(my_ids == other, grad_second, 0.0),
-        axis=1,
-        keepdims=True,
-    )
+
+    def gradient_of(ids):
+        at = lax.broadcasted_iota(jnp.int32, (ids.shape[0], resp), 1)
+        return jnp.sum(
+            jnp.where(ids == at, grad_first, 0.0) + jnp.where(ids == other, grad_second, 0.0),
+            axis=1,
+            keepdims=True,
+        )
+
     own = reward_sum[pl.ds(pl.multiple_of(me * 8, 8), 8)]
     for j in range(slots):
         rewards_out[j] = own[j, 0]
 
     def finish(r, g, k, v):
-        mine = jnp.sum(
-            jnp.where(slot_row[:, :1] == r, grads, 0.0), axis=0, keepdims=True
-        )
+        mine = gradient_of(jnp.full((LAST_ROWS, resp), me * slots + r, jnp.int32))
         up31 = dot(pick, stacked(up_buf, r, g), 1, 0)
         d31 = (up31 + mine * probe_of(g)).astype(jnp.bfloat16)
         dw = dot(d31, v, 1, 1)
         delta = jnp.sum(d31.astype(jnp.float32) * o_last[r, g], axis=1, keepdims=True)
         ds = (p_last[r, g] * (dw - delta) * scale).astype(jnp.bfloat16)
-        dk = d_rows[r, 2 * g] + dot(ds, q_last[r, g], 0, 0)
-        dv = d_rows[r, 2 * g + 1] + dot(w_last[r, g], d31, 0, 0)
+        dk = d_rows[r, 2 * g, prefix_len:] + dot(ds[:, prefix_len:], q_last[r, g], 0, 0)
+        dv = d_rows[r, 2 * g + 1, prefix_len:] + dot(w_last[r, g][:, prefix_len:], d31, 0, 0)
         dq = dot(pick, dot(ds, k, 1, 0).astype(jnp.bfloat16), 0, 0).astype(jnp.bfloat16)
         for h in range(group):
             cols = slice((g * group + h) * HD, (g * group + h + 1) * HD)
             gq_buf[r, :, cols] = gq_buf[r, :, cols] + dq[h * rows : (h + 1) * rows]
-        mine_rows = pl.ds(pl.multiple_of(r * rows, rows), rows)
-        grad_r_out[2 * g, mine_rows] = dk[prefix_len:].astype(jnp.bfloat16)
-        grad_r_out[2 * g + 1, mine_rows] = dv[prefix_len:].astype(jnp.bfloat16)
-        return dk[:prefix_len], dv[:prefix_len]
-
-    def backward_copy(chunk, kind):
-        src = (out_a, out_b, out_c, out_d)[kind].at[chunk]
-        dst = (in_a, in_b, in_c, in_d)[kind].at[chunk]
-        if kind < 2:
-            to = mate
-        elif kind == 2:
-            to = lax.rem(me + n_dp + 4 * odd - 2, n_dp)
-        else:
-            to = lax.rem(me + n_dp + 2 - 4 * odd, n_dp)
-        return pltpu.make_async_remote_copy(
-            src_ref=src,
-            dst_ref=dst,
-            send_sem=bwd_send.at[chunk, kind],
-            recv_sem=bwd_recv.at[chunk, kind],
-            device_id={"dp": to},
-            device_id_type=MESH,
-        )
-
-    bwd = [[backward_copy(c, k) for k in range(4)] for c in range(chunks)]
-    reach2 = offsets[0, 2]
-    reach3 = offsets[0, 3]
-
-    def part(d2, d3, reach):
-        return jnp.where(reach2 == reach, d2, 0.0) + jnp.where(reach3 == reach, d3, 0.0)
+        mine_rows = slice(r * rows, (r + 1) * rows)
+        grad_r_out[0, mine_rows, head(g)] = dk.astype(jnp.bfloat16)
+        grad_r_out[1, mine_rows, head(g)] = dv.astype(jnp.bfloat16)
 
     for g in range(heads_kv):
-        pairs = [finish(r, g, *far_keys(r, g)) for r in (2, 3)]
-        for c in range(2):
-            chunk = 2 * g + c
-            d2, d3 = pairs[0][c], pairs[1][c]
-            out_a[chunk] = part(d2, d3, 2 * odd - 1).astype(jnp.bfloat16)
-            bwd[chunk][0].start()
-            out_c[chunk] = part(d2, d3, 4 * odd - 2).astype(jnp.bfloat16)
-            bwd[chunk][2].start()
-            out_b[chunk] = part(d2, d3, 1 - 2 * odd).astype(jnp.bfloat16)
-            bwd[chunk][1].start()
-            d_rows[2, chunk, :prefix_len] = part(d2, d3, 0)
-            d_rows[3, chunk, :prefix_len] = part(d2, d3, 2 - 4 * odd)
-
-    for c in range(chunks):
-        bwd[c][0].wait_recv()
-        out_d[c] = (
-            d_rows[3, c, :prefix_len] + in_a[c].astype(jnp.float32)
-        ).astype(jnp.bfloat16)
-        bwd[c][3].start()
-
-    for g in range(heads_kv):
-        for r in (0, 1):
-            k, v = key_value(r, g, prefix[2 * g], prefix[2 * g + 1])
-            dk, dv = finish(r, g, k, v)
-            d_rows[2, 2 * g, :prefix_len] += dk
-            d_rows[2, 2 * g + 1, :prefix_len] += dv
+        for r in range(slots):
+            if r < 2:
+                finish(r, g, *key_value(r, g, prefix[0, :, head(g)], prefix[1, :, head(g)]))
+            else:
+                finish(r, g, *far_keys(r, g))
     store_q = pltpu.make_async_copy(gq_buf, grad_q_hbm, local_sem.at[2])
     store_q.start()
+
+    near_by = (0, 0, -1, 1, -2, 2)
+    pair_rows = lax.broadcasted_iota(jnp.int32, (2 * group, resp), 0)
+    second_slot = pair_rows >= group
+    grad_rows = []
+    used = []
+    for i, reach in enumerate(near_by):
+        device = lax.rem(me + n_dp + reach, n_dp)
+        first_slot = 0 if i == 0 else 2
+        ids = jnp.where(second_slot, 1, 0) + (device * slots + first_slot)
+        grad_rows.append(gradient_of(ids))
+        if i == 0:
+            used.append(jnp.ones((2 * group, 1), jnp.float32))
+        else:
+            told = table[device * n_tensor]
+            offset = jnp.where(
+                second_slot[:, :1], told[slots + 1 : slots + 2, :1], told[slots : slots + 1, :1]
+            )
+            used.append(jnp.where(offset == float(-reach), 1.0, 0.0))
+    grad_rows = jnp.concatenate(grad_rows, axis=0)
+    used = jnp.concatenate(used, axis=0)
+    for which in range(2):
+        for to in range(4):
+            notes[which][to].wait_recv()
+    stats = jnp.concatenate(
+        [stats_near[...], sent_stats[...]] + [got_stats[to] for to in range(4)], axis=0
+    )
+    for g in range(heads_kv):
+        q31 = jnp.concatenate(
+            [jnp.concatenate([q_last[0, g][:group], q_last[1, g][:group]], axis=0), sent_rows[0, g]]
+            + [got_rows[to, 0, g] for to in range(4)],
+            axis=0,
+        )
+        near_up = [dot(pick, stacked(up_buf, r, g), 1, 0)[:group] for r in (0, 1)]
+        up31 = jnp.concatenate(
+            near_up
+            + [sent_rows[1, g].astype(jnp.float32)]
+            + [got_rows[to, 1, g].astype(jnp.float32) for to in range(4)],
+            axis=0,
+        )
+        probes = jnp.concatenate([probe[g * group : (g + 1) * group]] * (2 * len(near_by)), axis=0)
+        top, inverse, up_o, probe_o = [stats[:, 4 * g + i : 4 * g + i + 1] for i in range(4)]
+        k, v = prefix[0, :, head(g)], prefix[1, :, head(g)]
+        d31 = (up31 + grad_rows * probes).astype(jnp.bfloat16)
+        w = jnp.where(used > 0.0, jnp.exp((dot(q31, k, 1, 1) - top) * scale) * inverse, 0.0)
+        dw = dot(d31, v, 1, 1)
+        ds = (w * (dw - (up_o + grad_rows * probe_o)) * scale).astype(jnp.bfloat16)
+        d_rows[2, 2 * g, :prefix_len] += (
+            d_rows[0, 2 * g, :prefix_len] + d_rows[1, 2 * g, :prefix_len] + dot(ds, q31, 0, 0)
+        )
+        d_rows[2, 2 * g + 1, :prefix_len] += (
+            d_rows[0, 2 * g + 1, :prefix_len]
+            + d_rows[1, 2 * g + 1, :prefix_len]
+            + dot(w.astype(jnp.bfloat16), d31, 0, 0)
+        )
 
     for c in range(chunks):
         bwd[c][1].wait_recv()
         bwd[c][2].wait_recv()
         bwd[c][3].wait_recv()
-        grad_p_out[c] = (
+        grad_p_out[c % 2, :, head(c // 2)] = (
             d_rows[2, c, :prefix_len]
             + in_b[c].astype(jnp.float32)
             + in_c[c].astype(jnp.float32)
@@ -404,6 +504,9 @@
         for k in range(4):
             fwd[c][k].wait_send()
             bwd[c][k].wait_send()
+    for which in range(2):
+        for to in range(4):
+            notes[which][to].wait_send()
     store_q.wait()
 
 
@@ -424,12 +527,12 @@
     kv_heads = response_cache.shape[3] // HD
     chunks = 2 * kv_heads
     keys = prefix_len + rows
+    group = width // HD // kv_heads
     resp = partner.shape[0]
     n_all = n_dp * n_tensor
-    prefix = prefix_cache.reshape(prefix_len, 2, kv_heads, HD).transpose(2, 1, 0, 3)
-    prefix = prefix.reshape(chunks, prefix_len, HD)
-    response = response_cache.reshape(slots * rows, 2, kv_heads, HD).transpose(2, 1, 0, 3)
-    response = response.reshape(chunks, slots * rows, HD)
+    kv_width = kv_heads * HD
+    prefix = prefix_cache[0].transpose(1, 0, 2)
+    response = response_cache.reshape(slots * rows, 2, kv_width).transpose(1, 0, 2)
     vmem = pl.BlockSpec(memory_space=pltpu.VMEM)
     smem = pl.BlockSpec(memory_space=pltpu.SMEM)
     hbm = pl.BlockSpec(memory_space=pl.ANY)
@@ -441,8 +544,8 @@
             jax.ShapeDtypeStruct((slots,), jnp.float32),
             jax.ShapeDtypeStruct((1,), jnp.float32),
             jax.ShapeDtypeStruct(queries.shape, jnp.bfloat16),
-            jax.ShapeDtypeStruct((chunks, slots * rows, HD), jnp.bfloat16),
-            jax.ShapeDtypeStruct((chunks, prefix_len, HD), jnp.bfloat16),
+            jax.ShapeDtypeStruct((2, slots * rows, kv_width), jnp.bfloat16),
+            jax.ShapeDtypeStruct((2, prefix_len, kv_width), jnp.bfloat16),
         ),
         in_specs=[smem, hbm, hbm, vmem, vmem, vmem, vmem, vmem],
         out_specs=(smem, smem, hbm, vmem, vmem),
@@ -462,6 +565,11 @@
             pltpu.VMEM((8, HD), jnp.float32),
             pltpu.VMEM((n_all, 8, HD), jnp.float32),
             pltpu.VMEM((n_dp * 8, HD), jnp.float32),
+            pltpu.VMEM((2, kv_heads, 2 * group, HD), jnp.bfloat16),
+            pltpu.VMEM((4, 2, kv_heads, 2 * group, HD), jnp.bfloat16),
+            pltpu.VMEM((2 * group, HD), jnp.float32),
+            pltpu.VMEM((4, 2 * group, HD), jnp.float32),
+            pltpu.VMEM((2 * group, HD), jnp.float32),
             block,
             block,
             block,
@@ -477,6 +585,8 @@
             pltpu.SemaphoreType.DMA((chunks, 4)),
             pltpu.SemaphoreType.DMA((n_all,)),
             pltpu.SemaphoreType.DMA((n_all,)),
+            pltpu.SemaphoreType.DMA((2, 4)),
+            pltpu.SemaphoreType.DMA((2, 4)),
         ],
         compiler_params=pltpu.CompilerParams(
             collective_id=0, has_side_effects=True, vmem_limit_bytes=40 * 1024 * 1024
@@ -491,8 +601,8 @@
         partner.reshape(1, resp),
         labels.reshape(1, resp),
     )
-    grad_response = grad_r.reshape(kv_heads, 2, slots, rows, HD).transpose(2, 3, 1, 0, 4)
-    grad_prefix = grad_p.reshape(kv_heads, 2, 1, prefix_len, HD).transpose(2, 3, 1, 0, 4)
+    grad_response = grad_r.transpose(1, 0, 2)
+    grad_prefix = grad_p.transpose(1, 0, 2)
     return (
         rewards,
         loss,

time: 53.2 us -> 46.1 us (0.87)
  Pallas kernels: 45.2 us -> 36.7 us
  local copies, waits for them, and re-layouts: 5.44 us -> 6.67 us
    pallas_call x1, Pallas kernels: 45.2 us -> 36.7 us  [per_device(): pl.pallas_call(functools.partial(kernel, n_dp, n_tensor), out_shape=(jax....]
    unnamed x16 -> x18, local copies, waits for them, and re-layouts: 2.25 us -> 6.67 us
    reshape x6 -> x0, local copies, waits for them, and re-layouts: 2.82 us -> none  [the longest x2 1.05 us: per_device(): response_cache.reshape(slots * rows, 2, kv_heads, HD).transpose(2, 1, 0, 3)]
where the time goes in v2:
time: 46.1 us; the launch traced here: 45.9 us
  Pallas kernels  36.7 us (80%)
  local copies, waits for them, and re-layouts  6.67 us (14%)
  between operations  2.53 us (5%)
    pallas_call x1, Pallas kernels, per_device(): pl.pallas_call(functools.partial(kernel, n_dp, n_tensor), out_shape=(jax....  36.7 us
    unnamed x18, local copies, waits for them, and re-layouts  6.67 us

profile of v2, /device:TPU:0, one launch (start us, length us, event | category | flops | bytes accessed | tf_op | source)
XLA Modules:
  0.0 45.9 jit_solution(3556077210545358762)
XLA Ops:
  0.6 0.0 copy-start
  0.6 1.0 %copy.14 = bf16[4,32,2,256]{3,1,0,2:T(8,128)(2,1)S(1)} copy(bf16[4,32,2,256]{3,2,1,0:T(2,128)(2,1)} %param.9) | data formatting | bytes 262144 | tf_op args[1]
  1.6 0.0 copy-start.2
  1.6 1.0 %copy.18 = bf16[1,224,2,256]{3,1,2,0:T(8,128)(2,1)S(1)} copy(bf16[1,224,2,256]{3,2,1,0:T(2,128)(2,1)} %param.10) | data formatting | bytes 458752 | tf_op args[2]
  2.6 0.0 copy-start.3
  2.6 0.0 copy-start.4
  2.6 0.0 copy-start.5
  2.6 0.0 copy-done
  2.7 0.0 copy-done.2
  2.7 0.6 %copy-done.3 = s32[1,4]{1,0:T(1,128)S(1)} copy-done((s32[1,4]{1,0:T(1,128)S(1)}, s32[1,4]{1,0:T(1,128)}, u32[]{:S(2)}) %copy-start.3) | copy-done | bytes 40
  3.3 0.0 copy-done.4
  3.3 0.0 copy-done.5
  3.3 0.0 copy-start.1
  3.3 1.0 %copy-done.1 = bf16[4,32,2048]{2,1,0:T(8,128)(2,1)S(1)} copy-done((bf16[4,32,2048]{2,1,0:T(8,128)(2,1)S(1)}, bf16[4,32,2048]{2,1,0:T(8,128)(2,1)}, u32[]{:S(2)}) %copy-start.1) | copy-done | bytes 524312
  4.3 36.7 %shard_map.119 = (f32[4]{0:T(128)S(1)}, f32[1]{0:T(128)}, bf16[4,32,2048]{2,1,0:T(8,128)(2,1)S(1)}, bf16[2,128,256]{2,1,0:T(8,128)(2,1)S(1)}, bf16[2,224,256]{2,1,0:T(8,128)(2,1)S(1)}) custom-call(s32[1,4]{1,0:T(1,128)S(1)} %copy-done.3, bf16[4,32,2048]{2,1,0:T(8,128)(2,1)S(1)} %copy-done, bf16[4,32,2048]{2,1,0:T(8,128)(2,1)S(1)} %copy-done.1, ...), custom_call_target="tpu_custom_call" | custom-call | tf_op jit(solution)/shard_map/pallas_call | solution.py:541
  41.0 0.8 %copy.15 = bf16[4,32,2,256]{3,2,1,0:T(2,128)(2,1)} copy(bf16[4,32,2,256]{3,1,0,2:T(8,128)(2,1)S(1)} %bitcast.20) | data formatting | bytes 262144
  41.8 0.9 %copy.16 = bf16[1,224,2,256]{3,2,1,0:T(2,128)(2,1)} copy(bf16[1,224,2,256]{3,1,2,0:T(8,128)(2,1)S(1)} %bitcast.19) | data formatting | bytes 458752
  42.7 0.5 %copy.22 = f32[4]{0:T(128)} copy(f32[4]{0:T(128)S(1)} %get-tuple-element.25) | data formatting | bytes 32
  43.9 0.8 %copy.24 = bf16[4,32,2048]{2,1,0:T(8,128)(2,1)} copy(bf16[4,32,2048]{2,1,0:T(8,128)(2,1)S(1)} %get-tuple-element.27) | data formatting | bytes 1048576
Async XLA Ops:
  0.6 2.0 %copy-start = (bf16[4,32,2048]{2,1,0:T(8,128)(2,1)S(1)}, bf16[4,32,2048]{2,1,0:T(8,128)(2,1)}, u32[]{:S(2)}) copy-start(bf16[4,32,2048]{2,1,0:T(8,128)(2,1)} %queries_hbm.1) | copy-start | bytes 1572868
  1.6 1.0 %copy-start.2 = (f32[2048]{0:T(1024)S(1)}, f32[2048]{0:T(1024)}, u32[]{:S(2)}) copy-start(f32[2048]{0:T(1024)} %param.12) | copy-start | bytes 24580
  2.6 0.7 %copy-start.3 = (s32[1,4]{1,0:T(1,128)S(1)}, s32[1,4]{1,0:T(1,128)}, u32[]{:S(2)}) copy-start(s32[1,4]{1,0:T(1,128)} %offsets.1) | copy-start | bytes 52
  2.6 0.7 %copy-start.4 = (s32[32]{0:T(128)S(1)}, s32[32]{0:T(128)}, u32[]{:S(2)}) copy-start(s32[32]{0:T(128)} %param.14) | copy-start | bytes 388
  2.6 0.7 %copy-start.5 = (s32[32]{0:T(128)S(1)}, s32[32]{0:T(128)}, u32[]{:S(2)}) copy-start(s32[32]{0:T(128)} %param.15) | copy-start | bytes 388
  3.3 1.0 %copy-start.1 = (bf16[4,32,2048]{2,1,0:T(8,128)(2,1)S(1)}, bf16[4,32,2048]{2,1,0:T(8,128)(2,1)}, u32[]{:S(2)}) copy-start(bf16[4,32,2048]{2,1,0:T(8,128)(2,1)} %upstream_hbm.1) | copy-start | bytes 1572868

commit v3 on v2

--- a/solution.py
+++ b/solution.py
@@ -23,19 +23,28 @@
 def kernel(
     n_dp,
     n_tensor,
-    offsets,
+    offsets_hbm,
     queries_hbm,
     upstream_hbm,
-    prefix,
-    response,
-    probe,
-    partner,
-    labels,
+    prefix_hbm,
+    response_hbm,
+    probe_hbm,
+    partner_hbm,
+    labels_hbm,
     rewards_out,
     loss_out,
     grad_q_hbm,
     grad_r_out,
     grad_p_out,
+    prefix_raw,
+    response_raw,
+    probe,
+    partner,
+    labels,
+    offsets,
+    prefix,
+    response,
+    grad_r,
     q_buf,
     up_buf,
     gq_buf,
@@ -88,8 +97,8 @@
     my_t = lax.axis_index("tensor")
     odd = lax.rem(me, 2)
     mate = me + 1 - 2 * odd
-    ahead = lax.rem(me + 2, n_dp)
-    behind = lax.rem(me + n_dp - 2, n_dp)
+    soon = lax.rem(me + n_dp - 2 + 4 * odd, n_dp)
+    later = lax.rem(me + n_dp + 2 - 4 * odd, n_dp)
     n_all = n_dp * n_tensor
     my_all = me * n_tensor + my_t
 
@@ -97,6 +106,21 @@
         other = lax.rem(my_all + step, n_all)
         return {"dp": lax.div(other, n_tensor), "tensor": lax.rem(other, n_tensor)}
 
+    loads = [
+        pltpu.make_async_copy(src, dst, local_sem.at[3 + i])
+        for i, (src, dst) in enumerate(
+            (
+                (prefix_hbm, prefix_raw),
+                (response_hbm, response_raw),
+                (probe_hbm, probe),
+                (offsets_hbm, offsets),
+                (partner_hbm, partner),
+                (labels_hbm, labels),
+            )
+        )
+    ]
+    for load in loads:
+        load.start()
     load_q = pltpu.make_async_copy(queries_hbm, q_buf, local_sem.at[0])
     load_up = pltpu.make_async_copy(upstream_hbm, up_buf, local_sem.at[1])
     load_q.start()
@@ -109,6 +133,8 @@
         return carry
 
     lax.fori_loop(1, n_all, greet, 0)
+    loads[0].wait()
+    prefix[...] = jnp.swapaxes(prefix_raw[0], 0, 1)
     pl.semaphore_wait(barrier, n_all - 1)
 
     def head(g):
@@ -121,9 +147,9 @@
         if kind == 0:
             src, dst, to = prefix_at(chunk), near[chunk].at[1 + 2 * odd], mate
         elif kind == 1:
-            src, dst, to = prefix_at(chunk), near[chunk].at[0], ahead
+            src, dst, to = prefix_at(chunk), near[chunk].at[4 - 4 * odd], soon
         elif kind == 2:
-            src, dst, to = prefix_at(chunk), near[chunk].at[4], behind
+            src, dst, to = prefix_at(chunk), near[chunk].at[4 * odd], later
         else:
             src, dst, to = near[chunk].at[4 - 4 * odd], near[chunk].at[3 - 2 * odd], mate
         return pltpu.make_async_remote_copy(
@@ -136,8 +162,8 @@
         )
 
     fwd = [[forward_copy(c, k) for k in range(4)] for c in range(chunks)]
-    for c in range(chunks):
-        for k in (1, 2, 0):
+    for k in (1, 0, 2):
+        for c in range(chunks):
             fwd[c][k].start()
 
     lane = lax.broadcasted_iota(jnp.int32, (1, m_len), 1)
@@ -219,6 +245,11 @@
     slot_row = lax.broadcasted_iota(jnp.int32, (8, HD), 0)
     lane_of = lax.broadcasted_iota(jnp.int32, (LAST_ROWS, HD), 1)
 
+    for load in loads[1:]:
+        load.wait()
+    response[...] = jnp.swapaxes(
+        response_raw[...].reshape(slots * rows, 2, kv_width), 0, 1
+    )
     load_q.wait()
     load_up.wait()
 
@@ -242,6 +273,8 @@
 
     notes = [[note_copy(which, to) for to in range(4)] for which in range(2)]
 
+    for c in range(chunks):
+        near[c][2] = prefix[c % 2, :, head(c // 2)]
     note = jnp.zeros((8, HD), jnp.float32)
     own_stats = []
     for r in (0, 1):
@@ -253,24 +286,11 @@
             mine = mine + packed
             main(r, g, k, v)
         own_stats.append(mine[:group])
-        if r == 0:
-            for c in range(chunks):
-                near[c][2] = prefix[c % 2, :, head(c // 2)]
+        for c in (2 * r, 2 * r + 1):
+            fwd[c][1].wait_recv()
+            fwd[c][3].start()
     stats_near[...] = jnp.concatenate(own_stats, axis=0)
 
-    def wait_arrival(c, kind, index):
-        pltpu.make_async_remote_copy(
-            src_ref=prefix_at(c),
-            dst_ref=near[c].at[index],
-            send_sem=fwd_send.at[c, kind],
-            recv_sem=fwd_recv.at[c, kind],
-            device_id={"dp": mate},
-            device_id_type=MESH,
-        ).wait_recv()
-
-    for c in range(chunks):
-        wait_arrival(c, 2 - odd, 4 - 4 * odd)
-        fwd[c][3].start()
     for to in range(4):
         notes[0][to].start()
 
@@ -280,9 +300,9 @@
         if kind < 2:
             to = mate
         elif kind == 2:
-            to = lax.rem(me + n_dp + 4 * odd - 2, n_dp)
+            to = soon
         else:
-            to = lax.rem(me + n_dp + 2 - 4 * odd, n_dp)
+            to = later
         return pltpu.make_async_remote_copy(
             src_ref=src,
             dst_ref=dst,
@@ -327,7 +347,7 @@
     far_stats = [jnp.zeros((LAST_ROWS, HD), jnp.float32)] * 2
     for g in range(heads_kv):
         for c in (2 * g, 2 * g + 1):
-            wait_arrival(c, 1 + odd, 4 * odd)
+            fwd[c][2].wait_recv()
             fwd[c][0].wait_recv()
             fwd[c][3].wait_recv()
         for r in (2, 3):
@@ -356,14 +376,13 @@
             out_c[chunk] = part(d2, d3, 4 * odd - 2).astype(jnp.bfloat16)
             bwd[chunk][2].start()
             out_b[chunk] = part(d2, d3, 1 - 2 * odd).astype(jnp.bfloat16)
-            bwd[chunk][1].start()
             d_rows[2, chunk, :prefix_len] = part(d2, d3, 0)
             d_rows[3, chunk, :prefix_len] = part(d2, d3, 2 - 4 * odd)
-        if g > 0:
-            pass_on(2 * g - 2)
-            pass_on(2 * g - 1)
-    pass_on(chunks - 2)
-    pass_on(chunks - 1)
+    for c in range(chunks):
+        pass_on(c)
+    for c in range(chunks):
+        bwd[c][0].wait_send()
+        bwd[c][1].start()
 
     def hear(step, carry):
         reward_copy(step).wait()
@@ -422,8 +441,8 @@
             cols = slice((g * group + h) * HD, (g * group + h + 1) * HD)
             gq_buf[r, :, cols] = gq_buf[r, :, cols] + dq[h * rows : (h + 1) * rows]
         mine_rows = slice(r * rows, (r + 1) * rows)
-        grad_r_out[0, mine_rows, head(g)] = dk.astype(jnp.bfloat16)
-        grad_r_out[1, mine_rows, head(g)] = dv.astype(jnp.bfloat16)
+        grad_r[0, mine_rows, head(g)] = dk.astype(jnp.bfloat16)
+        grad_r[1, mine_rows, head(g)] = dv.astype(jnp.bfloat16)
 
     for g in range(heads_kv):
         for r in range(slots):
@@ -431,6 +450,7 @@
                 finish(r, g, *key_value(r, g, prefix[0, :, head(g)], prefix[1, :, head(g)]))
             else:
                 finish(r, g, *far_keys(r, g))
+    grad_r_out[...] = jnp.swapaxes(grad_r[...], 0, 1).reshape(grad_r_out.shape)
     store_q = pltpu.make_async_copy(gq_buf, grad_q_hbm, local_sem.at[2])
     store_q.start()
 
@@ -490,10 +510,13 @@
         )
 
     for c in range(chunks):
+        for k in range(4):
+            fwd[c][k].wait_send()
+    for c in range(chunks):
         bwd[c][1].wait_recv()
         bwd[c][2].wait_recv()
         bwd[c][3].wait_recv()
-        grad_p_out[c % 2, :, head(c // 2)] = (
+        prefix[c % 2, :, head(c // 2)] = (
             d_rows[2, c, :prefix_len]
             + in_b[c].astype(jnp.float32)
             + in_c[c].astype(jnp.float32)
@@ -501,9 +524,9 @@
         ).astype(jnp.bfloat16)
 
     for c in range(chunks):
-        for k in range(4):
-            fwd[c][k].wait_send()
+        for k in (1, 2, 3):
             bwd[c][k].wait_send()
+    grad_p_out[...] = jnp.swapaxes(prefix[...], 0, 1)[None]
     for which in range(2):
         for to in range(4):
             notes[which][to].wait_send()
@@ -531,8 +554,7 @@
     resp = partner.shape[0]
     n_all = n_dp * n_tensor
     kv_width = kv_heads * HD
-    prefix = prefix_cache[0].transpose(1, 0, 2)
-    response = response_cache.reshape(slots * rows, 2, kv_width).transpose(1, 0, 2)
+    kv_width = kv_heads * HD
     vmem = pl.BlockSpec(memory_space=pltpu.VMEM)
     smem = pl.BlockSpec(memory_space=pltpu.SMEM)
     hbm = pl.BlockSpec(memory_space=pl.ANY)
@@ -544,12 +566,21 @@
             jax.ShapeDtypeStruct((slots,), jnp.float32),
             jax.ShapeDtypeStruct((1,), jnp.float32),
             jax.ShapeDtypeStruct(queries.shape, jnp.bfloat16),
-            jax.ShapeDtypeStruct((2, slots * rows, kv_width), jnp.bfloat16),
-            jax.ShapeDtypeStruct((2, prefix_len, kv_width), jnp.bfloat16),
+            jax.ShapeDtypeStruct(response_cache.shape, jnp.bfloat16),
+            jax.ShapeDtypeStruct(prefix_cache.shape, jnp.bfloat16),
         ),
-        in_specs=[smem, hbm, hbm, vmem, vmem, vmem, vmem, vmem],
+        in_specs=[hbm] * 8,
         out_specs=(smem, smem, hbm, vmem, vmem),
         scratch_shapes=[
+            pltpu.VMEM(prefix_cache.shape, jnp.bfloat16),
+            pltpu.VMEM(response_cache.shape, jnp.bfloat16),
+            pltpu.VMEM((width // HD, HD), jnp.float32),
+            pltpu.VMEM((1, resp), jnp.int32),
+            pltpu.VMEM((1, resp), jnp.int32),
+            pltpu.SMEM((1, slots), jnp.int32),
+            pltpu.VMEM((2, prefix_len, kv_width), jnp.bfloat16),
+            pltpu.VMEM((2, slots * rows, kv_width), jnp.bfloat16),
+            pltpu.VMEM((2, slots * rows, kv_width), jnp.bfloat16),
             pltpu.VMEM(queries.shape, jnp.bfloat16),
             pltpu.VMEM(queries.shape, jnp.bfloat16),
             pltpu.VMEM(queries.shape, jnp.bfloat16),
@@ -578,7 +609,7 @@
             block,
             block,
             block,
-            pltpu.SemaphoreType.DMA((3,)),
+            pltpu.SemaphoreType.DMA((9,)),
             pltpu.SemaphoreType.DMA((chunks, 4)),
             pltpu.SemaphoreType.DMA((chunks, 4)),
             pltpu.SemaphoreType.DMA((chunks, 4)),
@@ -589,27 +620,19 @@
             pltpu.SemaphoreType.DMA((2, 4)),
         ],
         compiler_params=pltpu.CompilerParams(
-            collective_id=0, has_side_effects=True, vmem_limit_bytes=40 * 1024 * 1024
+            collective_id=0, has_side_effects=True, vmem_limit_bytes=60 * 1024 * 1024
         ),
     )(
         slot_offsets,
         queries,
         upstream,
-        prefix,
-        response,
+        prefix_cache,
+        response_cache,
         reward_probe.reshape(width // HD, HD),
         partner.reshape(1, resp),
         labels.reshape(1, resp),
     )
-    grad_response = grad_r.transpose(1, 0, 2)
-    grad_prefix = grad_p.transpose(1, 0, 2)
-    return (
-        rewards,
-        loss,
-        grad_q,
-        grad_response.reshape(response_cache.shape),
-        grad_prefix.reshape(prefix_cache.shape),
-    )
+    return rewards, loss, grad_q, grad_r, grad_p
 
 
 def solution(mesh):

time: 46.1 us -> 40.1 us (0.87)
  Pallas kernels: 36.7 us -> 32.7 us
  local copies, waits for them, and re-layouts: 6.67 us -> 4.76 us
    pallas_call x1, Pallas kernels: 36.7 us -> 32.7 us  [per_device(): pl.pallas_call(functools.partial(kernel, n_dp, n_tensor), out_shape=(jax....]
    unnamed x18 -> x10, local copies, waits for them, and re-layouts: 6.67 us -> 4.76 us
where the time goes in v3:
time: 40.1 us; the launch traced here: 39.9 us
  Pallas kernels  32.7 us (82%)
  local copies, waits for them, and re-layouts  4.76 us (12%)
  between operations  2.43 us (6%)
    pallas_call x1, Pallas kernels, per_device(): pl.pallas_call(functools.partial(kernel, n_dp, n_tensor), out_shape=(jax....  32.7 us
    unnamed x10, local copies, waits for them, and re-layouts  4.76 us

profile of v3, /device:TPU:0, one launch (start us, length us, event | category | flops | bytes accessed | tf_op | source)
XLA Modules:
  0.0 39.9 jit_solution(10523142863256081886)
XLA Ops:
  0.6 32.7 %shard_map.119 = (f32[4]{0:T(128)}, f32[1]{0:T(128)}, bf16[4,32,2048]{2,1,0:T(8,128)(2,1)}, bf16[4,32,2,256]{3,2,1,0:T(2,128)(2,1)}, bf16[1,224,2,256]{3,2,1,0:T(2,128)(2,1)}) custom-call(s32[1,4]{1,0:T(1,128)} %offsets_hbm.1, bf16[4,32,2048]{2,1,0:T(8,128)(2,1)} %queries_hbm.1, bf16[4,32,2048]{2,1,0:T(8,128)(2,1)} %upstream_hbm.1, ...), custom_call_target="tpu_custom_call" | custom-call | tf_op jit(solution)/shard_map/pallas_call | solution.py:563
  33.4 0.0 copy-start.2
  33.4 0.7 %copy-done.2 = f32[4]{0:T(128)S(1)} copy-done((f32[4]{0:T(128)S(1)}, f32[4]{0:T(128)}, u32[]{:S(2)}) %copy-start.2) | copy-done | bytes 40
  34.0 0.5 %copy.18 = f32[4]{0:T(128)} copy(f32[4]{0:T(128)S(1)} %copy-done.2) | data formatting | bytes 32
  35.2 0.0 copy-start.1
  35.2 1.9 %copy.20 = bf16[4,32,2048]{2,1,0:T(8,128)(2,1)} copy(bf16[4,32,2048]{2,1,0:T(8,128)(2,1)} %get-tuple-element.12) | data formatting | bytes 1048576
  37.1 0.0 copy-done.1
  37.1 0.0 copy-start
  37.1 0.7 %copy.21 = bf16[4,32,2,256]{3,2,1,0:T(2,128)(2,1)} copy(bf16[4,32,2,256]{3,2,1,0:T(2,128)(2,1)S(1)} %copy-done.1) | data formatting | bytes 262144
  37.8 0.3 copy-done
  38.1 0.7 %copy.22 = bf16[1,224,2,256]{3,2,1,0:T(2,128)(2,1)} copy(bf16[1,224,2,256]{3,2,1,0:T(2,128)(2,1)S(1)} %copy-done) | data formatting | bytes 458752
Async XLA Ops:
  33.4 0.7 %copy-start.2 = (f32[4]{0:T(128)S(1)}, f32[4]{0:T(128)}, u32[]{:S(2)}) copy-start(f32[4]{0:T(128)} %get-tuple-element.10) | copy-start | bytes 52
  35.2 1.9 %copy-start.1 = (bf16[4,32,2,256]{3,2,1,0:T(2,128)(2,1)S(1)}, bf16[4,32,2,256]{3,2,1,0:T(2,128)(2,1)}, u32[]{:S(2)}) copy-start(bf16[4,32,2,256]{3,2,1,0:T(2,128)(2,1)} %get-tuple-element.13) | copy-start | bytes 393220
  37.1 1.0 %copy-start = (bf16[1,224,2,256]{3,2,1,0:T(2,128)(2,1)S(1)}, bf16[1,224,2,256]{3,2,1,0:T(2,128)(2,1)}, u32[]{:S(2)}) copy-start(bf16[1,224,2,256]{3,2,1,0:T(2,128)(2,1)} %get-tuple-element.14) | copy-start | bytes 688132

commit v4 on v3

--- a/solution.py
+++ b/solution.py
@@ -533,6 +533,16 @@
     store_q.wait()
 
 
+def hand_over(*refs):
+    count = len(refs) // 2
+    for i in range(count):
+        if refs[i].ndim > 1:
+            refs[count + i][...] = refs[i][...]
+        else:
+            for j in range(refs[i].shape[0]):
+                refs[count + i][j] = refs[i][j]
+
+
 def per_device(
     n_dp,
     n_tensor,
@@ -632,7 +642,18 @@
         partner.reshape(1, resp),
         labels.reshape(1, resp),
     )
-    return rewards, loss, grad_q, grad_r, grad_p
+    results = [rewards, loss, grad_q, grad_r, grad_p]
+    moved = (0, 1, 2, 3, 4)
+    taken = [results[i] for i in moved]
+    given = pl.pallas_call(
+        hand_over,
+        out_shape=tuple(jax.ShapeDtypeStruct(x.shape, x.dtype) for x in taken),
+        in_specs=[smem if x.ndim == 1 else vmem for x in taken],
+        out_specs=tuple(smem if x.ndim == 1 else vmem for x in taken),
+    )(*taken)
+    for i, value in zip(moved, given):
+        results[i] = value
+    return tuple(results)
 
 
 def solution(mesh):

time: 40.1 us -> 36.3 us (0.905)
  local copies, waits for them, and re-layouts: 4.76 us -> 0 us
  Pallas kernels: 32.7 us -> 35.5 us
  between operations: 2.43 us -> 0.64 us
    unnamed x10 -> x0, local copies, waits for them, and re-layouts: 4.76 us -> none
    pallas_call x0 -> x1, Pallas kernels: none -> 2.7 us  [per_device(): pl.pallas_call(hand_over, out_shape=tuple((jax.ShapeDtypeStruct(x.shape,...]
where the time goes in v4:
time: 36.3 us; the launch traced here: 36.1 us
  Pallas kernels  35.5 us (98%)
  between operations  0.64 us (2%)
    pallas_call x1, Pallas kernels, per_device(): pl.pallas_call(functools.partial(kernel, n_dp, n_tensor), out_shape=(jax....  32.8 us
    pallas_call x1, Pallas kernels, per_device(): pl.pallas_call(hand_over, out_shape=tuple((jax.ShapeDtypeStruct(x.shape,...  2.7 us

profile of v4, /device:TPU:0, one launch (start us, length us, event | category | flops | bytes accessed | tf_op | source)
XLA Modules:
  0.0 36.1 jit_solution(17501567982146751290)
XLA Ops:
  0.6 32.8 %shard_map.119 = (f32[4]{0:T(128)}, f32[1]{0:T(128)}, bf16[4,32,2048]{2,1,0:T(8,128)(2,1)}, bf16[4,32,2,256]{3,2,1,0:T(2,128)(2,1)}, bf16[1,224,2,256]{3,2,1,0:T(2,128)(2,1)}) custom-call(s32[1,4]{1,0:T(1,128)} %offsets_hbm.1, bf16[4,32,2048]{2,1,0:T(8,128)(2,1)} %queries_hbm.1, bf16[4,32,2048]{2,1,0:T(8,128)(2,1)} %upstream_hbm.1, ...), custom_call_target="tpu_custom_call" | custom-call | tf_op jit(solution)/shard_map/pallas_call | solution.py:573
  33.4 2.7 %shard_map.120 = (f32[4]{0:T(128)}, f32[1]{0:T(128)}, bf16[4,32,2048]{2,1,0:T(8,128)(2,1)}, bf16[4,32,2,256]{3,2,1,0:T(2,128)(2,1)}, bf16[1,224,2,256]{3,2,1,0:T(2,128)(2,1)}) custom-call(f32[4]{0:T(128)} %get-tuple-element.10.refs_0_, f32[1]{0:T(128)} %get-tuple-element.11.refs_1_, bf16[4,32,2048]{2,1,0:T(8,128)(2,1)} %get-tuple-element.12.refs_2_, ...), custom_call_target="tpu_custom_call" | custom-call | tf_op jit(solution)/shard_map/pallas_call | solution.py:648

commit v5 on v4

--- a/solution.py
+++ b/solution.py
@@ -57,6 +57,7 @@
     p_last,
     o_last,
     q_last,
+    u_last,
     message,
     table,
     reward_sum,
@@ -209,11 +210,13 @@
         w_last[r, g] = w_low
         p_last[r, g] = w
         o_last[r, g] = o
+        up31 = dot(pick, stacked(up_buf, r, g), 1, 0)
+        u_last[r, g] = up31
         by_head = jnp.sum(o * probe_of(g), axis=1, keepdims=True)
         stats = [
             jnp.max(s, axis=1, keepdims=True),
             1.0 / jnp.sum(e, axis=1, keepdims=True),
-            jnp.sum(o * dot(pick, stacked(up_buf, r, g), 1, 0), axis=1, keepdims=True),
+            jnp.sum(o * up31, axis=1, keepdims=True),
             by_head,
         ]
         packed = jnp.zeros((LAST_ROWS, HD), jnp.float32)
@@ -427,19 +430,23 @@
     for j in range(slots):
         rewards_out[j] = own[j, 0]
 
+    last_of_tile = lax.broadcasted_iota(jnp.int32, (16, HD), 0) == 15
+
     def finish(r, g, k, v):
         mine = gradient_of(jnp.full((LAST_ROWS, resp), me * slots + r, jnp.int32))
-        up31 = dot(pick, stacked(up_buf, r, g), 1, 0)
-        d31 = (up31 + mine * probe_of(g)).astype(jnp.bfloat16)
+        d31 = (u_last[r, g] + mine * probe_of(g)).astype(jnp.bfloat16)
         dw = dot(d31, v, 1, 1)
         delta = jnp.sum(d31.astype(jnp.float32) * o_last[r, g], axis=1, keepdims=True)
         ds = (p_last[r, g] * (dw - delta) * scale).astype(jnp.bfloat16)
         dk = d_rows[r, 2 * g, prefix_len:] + dot(ds[:, prefix_len:], q_last[r, g], 0, 0)
         dv = d_rows[r, 2 * g + 1, prefix_len:] + dot(w_last[r, g][:, prefix_len:], d31, 0, 0)
-        dq = dot(pick, dot(ds, k, 1, 0).astype(jnp.bfloat16), 0, 0).astype(jnp.bfloat16)
+        dq = dot(ds, k, 1, 0)
         for h in range(group):
             cols = slice((g * group + h) * HD, (g * group + h + 1) * HD)
-            gq_buf[r, :, cols] = gq_buf[r, :, cols] + dq[h * rows : (h + 1) * rows]
+            old = gq_buf[r, rows - 16 :, cols].astype(jnp.float32)
+            gq_buf[r, rows - 16 :, cols] = jnp.where(
+                last_of_tile, dq[h : h + 1], old
+            ).astype(jnp.bfloat16)
         mine_rows = slice(r * rows, (r + 1) * rows)
         grad_r[0, mine_rows, head(g)] = dk.astype(jnp.bfloat16)
         grad_r[1, mine_rows, head(g)] = dv.astype(jnp.bfloat16)
@@ -486,7 +493,7 @@
             + [got_rows[to, 0, g] for to in range(4)],
             axis=0,
         )
-        near_up = [dot(pick, stacked(up_buf, r, g), 1, 0)[:group] for r in (0, 1)]
+        near_up = [u_last[r, g][:group] for r in (0, 1)]
         up31 = jnp.concatenate(
             near_up
             + [sent_rows[1, g].astype(jnp.float32)]
@@ -603,6 +610,7 @@
             pltpu.VMEM((slots, kv_heads, LAST_ROWS, keys), jnp.float32),
             pltpu.VMEM((slots, kv_heads, LAST_ROWS, HD), jnp.float32),
             pltpu.VMEM((slots, kv_heads, LAST_ROWS, HD), jnp.bfloat16),
+            pltpu.VMEM((slots, kv_heads, LAST_ROWS, HD), jnp.float32),
             pltpu.VMEM((8, HD), jnp.float32),
             pltpu.VMEM((n_all, 8, HD), jnp.float32),
             pltpu.VMEM((n_dp * 8, HD), jnp.float32),

time: 36.3 us -> 36.2 us (level)
  no operation moved by 1% of the time
where the time goes in v5:
time: 36.2 us; the launch traced here: 36.1 us
  Pallas kernels  35.4 us (98%)
  between operations  0.64 us (2%)
    pallas_call x1, Pallas kernels, per_device(): pl.pallas_call(functools.partial(kernel, n_dp, n_tensor), out_shape=(jax....  32.7 us
    pallas_call x1, Pallas kernels, per_device(): pl.pallas_call(hand_over, out_shape=tuple((jax.ShapeDtypeStruct(x.shape,...  2.7 us

profile of v5, /device:TPU:0, one launch (start us, length us, event | category | flops | bytes accessed | tf_op | source)
XLA Modules:
  0.0 36.1 jit_solution(823279371269028421)
XLA Ops:
  0.6 32.7 %shard_map.119 = (f32[4]{0:T(128)}, f32[1]{0:T(128)}, bf16[4,32,2048]{2,1,0:T(8,128)(2,1)}, bf16[4,32,2,256]{3,2,1,0:T(2,128)(2,1)}, bf16[1,224,2,256]{3,2,1,0:T(2,128)(2,1)}) custom-call(s32[1,4]{1,0:T(1,128)} %offsets_hbm.1, bf16[4,32,2048]{2,1,0:T(8,128)(2,1)} %queries_hbm.1, bf16[4,32,2048]{2,1,0:T(8,128)(2,1)} %upstream_hbm.1, ...), custom_call_target="tpu_custom_call" | custom-call | tf_op jit(solution)/shard_map/pallas_call | solution.py:580
  33.4 2.7 %shard_map.120 = (f32[4]{0:T(128)}, f32[1]{0:T(128)}, bf16[4,32,2048]{2,1,0:T(8,128)(2,1)}, bf16[4,32,2,256]{3,2,1,0:T(2,128)(2,1)}, bf16[1,224,2,256]{3,2,1,0:T(2,128)(2,1)}) custom-call(f32[4]{0:T(128)} %get-tuple-element.10.refs_0_, f32[1]{0:T(128)} %get-tuple-element.11.refs_1_, bf16[4,32,2048]{2,1,0:T(8,128)(2,1)} %get-tuple-element.12.refs_2_, ...), custom_call_target="tpu_custom_call" | custom-call | tf_op jit(solution)/shard_map/pallas_call | solution.py:656
